TPU v7x, 32 devices: a whole 2x2x4 slice. The times are simulated.
32 devices in a mesh: replica: 4 (over x, core), shard: 8 (over z, y).
Axes of the slice: x: 2, y: 2, z: 4, core: 2. Of those that a mesh axis runs over, the one named last changes fastest.
Arguments:
- tokens: bfloat16 [32768, 768], P(('replica', 'shard')), may hold values from -6 to 6
- gain_attn: bfloat16 [768], P('shard'), may hold values from 0.099609375 to 1.8984375
- w_qkv: bfloat16 [768, 2304], P('shard'), may hold values from -0.3125 to 0.3125
- w_out: bfloat16 [768, 768], P('shard'), may hold values from -0.875 to 0.875
- gain_ffn: bfloat16 [768], P('shard'), may hold values from 0.099609375 to 1.8984375
- w_in: bfloat16 [768, 2304], P('shard'), may hold values from -0.21875 to 0.21875
- w_down: bfloat16 [1152, 768], P('shard'), may hold values from -0.1875 to 0.1875
- cotangent: bfloat16 [32768, 768], P(('replica', 'shard')), may hold values from -6 to 6
Outputs:
- output: bfloat16 [32768, 768], P(('replica', 'shard'))
- input_grad: bfloat16 [32768, 768], P(('replica', 'shard'))
- grad_gain_attn: float32 [768], P('shard')
- grad_qkv: float32 [768, 2304], P('shard')
- grad_out: float32 [768, 768], P('shard')
- grad_gain_ffn: float32 [768], P('shard')
- grad_in: float32 [768, 2304], P('shard')
- grad_down: float32 [1152, 768], P('shard')
All inputs are finite; a program needn't handle non-finite values.
Results may differ from a plain program's by a relative error of at most 0.018.
Values may be sent and summed in bfloat16 or wider, within the bound.
A program may use at most 128 MiB of HBM per device.

v0:
```python
import math

import jax
import jax.numpy as jnp
from jax import lax
from jax.sharding import PartitionSpec as P

D = 768
HEADS = 12
HEAD_DIM = 64
FF = 1152
WINDOW = 128
LENGTH = 1024


epsilon = 1e-05


def normalize(values):
    centre = values - jnp.mean(values, axis=-1, keepdims=True)
    inverse = lax.rsqrt(jnp.mean(centre * centre, axis=-1, keepdims=True) + epsilon)
    return (centre * inverse, inverse)


def norm_back(grad_norm, standard, inverse, gain):
    scaled = grad_norm * gain
    return inverse * (
        scaled
        - jnp.mean(scaled, axis=-1, keepdims=True)
        - standard * jnp.mean(scaled * standard, axis=-1, keepdims=True)
    )


def rotary_tables(count):
    half_dim = HEAD_DIM // 2
    freqs = 10000.0 ** (-(jnp.arange(half_dim, dtype=jnp.float32) * 2.0) / HEAD_DIM)
    places = (jnp.arange(count, dtype=jnp.int32) % LENGTH).astype(jnp.float32)
    angles = places[:, None] * freqs[None, :]
    angles = jnp.concatenate([angles, angles], axis=1)
    return (jnp.cos(angles)[:, None, :], jnp.sin(angles)[:, None, :])


def rotate_half(values):
    half_dim = values.shape[-1] // 2
    return jnp.concatenate([-values[..., half_dim:], values[..., :half_dim]], axis=-1)


def rotate_back(values):
    half_dim = values.shape[-1] // 2
    return jnp.concatenate([values[..., half_dim:], -values[..., :half_dim]], axis=-1)


def windows(field, block_rows, margin):
    seq_count = field.shape[0] // LENGTH
    blocks = LENGTH // block_rows
    shaped = field.reshape(seq_count, LENGTH, HEADS, HEAD_DIM)
    padded = jnp.pad(shaped, ((0, 0), (margin, block_rows - margin), (0, 0), (0, 0)))
    first = padded[:, :LENGTH].reshape(seq_count, blocks, block_rows, HEADS, HEAD_DIM)
    second = padded[:, block_rows : block_rows + LENGTH].reshape(
        seq_count, blocks, block_rows, HEADS, HEAD_DIM
    )
    joined = jnp.concatenate([first, second[:, :, : 2 * margin]], axis=2)
    return joined.reshape(seq_count * blocks, block_rows + 2 * margin, HEADS, HEAD_DIM)


def unwindow(field, block_rows, margin):
    blocks = LENGTH // block_rows
    seq_count = field.shape[0] // blocks
    shaped = field.reshape(seq_count, blocks, block_rows + 2 * margin, HEADS, HEAD_DIM)
    first = shaped[:, :, :block_rows].reshape(seq_count, LENGTH, HEADS, HEAD_DIM)
    second = jnp.pad(
        shaped[:, :, block_rows:], ((0, 0), (0, 0), (0, block_rows - 2 * margin), (0, 0), (0, 0))
    )
    second = second.reshape(seq_count, LENGTH, HEADS, HEAD_DIM)
    whole = jnp.pad(first, ((0, 0), (0, block_rows), (0, 0), (0, 0))) + jnp.pad(
        second, ((0, 0), (block_rows, 0), (0, 0), (0, 0))
    )
    return whole[:, margin : margin + LENGTH].reshape(seq_count * LENGTH, HEADS, HEAD_DIM)


def to_items(field):
    per_group = math.gcd(HEADS, 4)
    head_groups = HEADS // per_group
    count, rows = (field.shape[0], field.shape[1])
    shaped = field.reshape(count, rows, head_groups, per_group, HEAD_DIM).transpose(0, 2, 1, 3, 4)
    return shaped.reshape(count * head_groups, rows, per_group, HEAD_DIM)


def from_items(field):
    per_group = math.gcd(HEADS, 4)
    head_groups = HEADS // per_group
    count, rows = (field.shape[0] // head_groups, field.shape[1])
    shaped = field.reshape(count, head_groups, rows, per_group, HEAD_DIM).transpose(0, 2, 1, 3, 4)
    return shaped.reshape(count, rows, HEADS, HEAD_DIM)


def block_scores(query_part, key_part, start, block_rows, margin):
    span = key_part.shape[0]
    query_pos = start + jnp.arange(block_rows, dtype=jnp.int32)[:, None]
    key_pos = start - margin + jnp.arange(span, dtype=jnp.int32)[None, :]
    allowed = (key_pos >= 0) & (key_pos < LENGTH) & (jnp.abs(query_pos - key_pos) <= margin)
    raw = jnp.einsum(
        "qhd,khd->hqk", query_part, key_part, preferred_element_type=jnp.float32
    ) * HEAD_DIM ** (-0.5)
    return jnp.where(allowed[None], raw, -1e30)


def block_starts(count, block_rows):
    per_group = math.gcd(HEADS, 4)
    blocks = LENGTH // block_rows
    starts = jnp.arange(count, dtype=jnp.int32) % blocks * block_rows
    return jnp.repeat(starts, HEADS // per_group)


def attend_forward(queries, keys, values):
    count_tok = queries.shape[0]
    block_rows = min(512, LENGTH)
    margin = WINDOW // 2
    query_items = to_items(queries.reshape(count_tok // block_rows, block_rows, HEADS, HEAD_DIM))
    key_items = to_items(windows(keys, block_rows, margin))
    value_items = to_items(windows(values, block_rows, margin))
    starts = block_starts(count_tok // block_rows, block_rows)

    def one_block(pieces):
        query_part, key_part, value_part, start = pieces
        scores = block_scores(query_part, key_part, start, block_rows, margin)
        top = jnp.max(scores, axis=-1, keepdims=True)
        expo = jnp.exp(scores - top)
        total = jnp.sum(expo, axis=-1, keepdims=True)
        probs = (expo / total).astype(jnp.bfloat16)
        mixed = jnp.einsum("hqk,khd->qhd", probs, value_part, preferred_element_type=jnp.float32)
        return (mixed.astype(jnp.bfloat16), top[..., 0] + jnp.log(total[..., 0]))

    mixed, log_totals = lax.map(one_block, (query_items, key_items, value_items, starts))
    return (from_items(mixed).reshape(count_tok, D), log_totals)


def attend_backward(queries, keys, values, grad_mixed, log_totals):
    count_tok = queries.shape[0]
    block_rows = min(512, LENGTH)
    margin = WINDOW // 2
    scale = HEAD_DIM ** (-0.5)
    query_items = to_items(queries.reshape(count_tok // block_rows, block_rows, HEADS, HEAD_DIM))
    grad_items = to_items(grad_mixed.reshape(count_tok // block_rows, block_rows, HEADS, HEAD_DIM))
    key_items = to_items(windows(keys, block_rows, margin))
    value_items = to_items(windows(values, block_rows, margin))
    starts = block_starts(count_tok // block_rows, block_rows)

    def one_block(pieces):
        query_part, key_part, value_part, grad_part, log_part, start = pieces
        scores = block_scores(query_part, key_part, start, block_rows, margin)
        probs = jnp.exp(scores - log_part[..., None])
        grad_probs = jnp.einsum(
            "qhd,khd->hqk", grad_part, value_part, preferred_element_type=jnp.float32
        )
        centre = jnp.sum(grad_probs * probs, axis=-1, keepdims=True)
        grad_scores = (probs * (grad_probs - centre)).astype(jnp.bfloat16)
        grad_query = (
            jnp.einsum("hqk,khd->qhd", grad_scores, key_part, preferred_element_type=jnp.float32)
            * scale
        )
        grad_key = (
            jnp.einsum("hqk,qhd->khd", grad_scores, query_part, preferred_element_type=jnp.float32)
            * scale
        )
        grad_value = jnp.einsum(
            "hqk,qhd->khd",
            probs.astype(jnp.bfloat16),
            grad_part,
            preferred_element_type=jnp.float32,
        )
        return (grad_query, grad_key, grad_value)

    grad_query, grad_key, grad_value = lax.map(
        one_block, (query_items, key_items, value_items, grad_items, log_totals, starts)
    )
    grad_query = from_items(grad_query).reshape(count_tok, HEADS, HEAD_DIM)
    grad_key = unwindow(from_items(grad_key), block_rows, margin)
    grad_value = unwindow(from_items(grad_value), block_rows, margin)
    return (grad_query, grad_key, grad_value)


def body(tokens, gain_attn, w_qkv, w_out, gain_ffn, w_in, w_down, cotangent):
    count_tok = tokens.shape[0]
    gain_one, joint_weight, out_weight = (
        lax.all_gather(gain_attn, "shard", axis=0, tiled=True),
        lax.all_gather(w_qkv, "shard", axis=0, tiled=True),
        lax.all_gather(w_out, "shard", axis=0, tiled=True),
    )
    gain_two, in_weight, down_weight = (
        lax.all_gather(gain_ffn, "shard", axis=0, tiled=True),
        lax.all_gather(w_in, "shard", axis=0, tiled=True),
        lax.all_gather(w_down, "shard", axis=0, tiled=True),
    )
    stream = tokens.astype(jnp.float32)
    standard_one, inverse_one = normalize(stream)
    normed_attn = (standard_one * gain_one.astype(jnp.float32)).astype(jnp.bfloat16)
    projected = jnp.dot(normed_attn, joint_weight, preferred_element_type=jnp.float32)
    projected = projected.reshape(count_tok, 3, HEADS, HEAD_DIM)
    cosine, sine = rotary_tables(count_tok)
    raw_query = projected[:, 0]
    raw_key = projected[:, 1]
    queries = (raw_query * cosine + rotate_half(raw_query) * sine).astype(jnp.bfloat16)
    keys = (raw_key * cosine + rotate_half(raw_key) * sine).astype(jnp.bfloat16)
    values = projected[:, 2].astype(jnp.bfloat16)
    attended, log_totals = attend_forward(queries, keys, values)
    after_attn = stream + jnp.dot(attended, out_weight, preferred_element_type=jnp.float32)
    standard_two, inverse_two = normalize(after_attn)
    normed_ffn = (standard_two * gain_two.astype(jnp.float32)).astype(jnp.bfloat16)
    gate_up = jnp.dot(normed_ffn, in_weight, preferred_element_type=jnp.float32)
    lifted = gate_up[:, :FF]
    gate_part = gate_up[:, FF:]
    normal_cdf = 0.5 * (1.0 + lax.erf(lifted * 0.7071067811865476))
    gelu_value = lifted * normal_cdf
    activated = (gelu_value * gate_part).astype(jnp.bfloat16)
    final = after_attn + jnp.dot(activated, down_weight, preferred_element_type=jnp.float32)
    output = final.astype(jnp.bfloat16)
    gain_one, joint_weight, out_weight = (
        lax.all_gather(gain_attn, "shard", axis=0, tiled=True),
        lax.all_gather(w_qkv, "shard", axis=0, tiled=True),
        lax.all_gather(w_out, "shard", axis=0, tiled=True),
    )
    gain_two, in_weight, down_weight = (
        lax.all_gather(gain_ffn, "shard", axis=0, tiled=True),
        lax.all_gather(w_in, "shard", axis=0, tiled=True),
        lax.all_gather(w_down, "shard", axis=0, tiled=True),
    )
    grad_final = cotangent.astype(jnp.float32)
    grad_down = jnp.einsum("tf,td->fd", activated, cotangent, preferred_element_type=jnp.float32)
    grad_act = jnp.einsum("td,fd->tf", cotangent, down_weight, preferred_element_type=jnp.float32)
    density = jnp.exp(-0.5 * lifted * lifted) * 0.3989422804014327
    grad_lifted = grad_act * gate_part * (normal_cdf + lifted * density)
    grad_gate = grad_act * gelu_value
    grad_gate_up = jnp.concatenate([grad_lifted, grad_gate], axis=1).astype(jnp.bfloat16)
    grad_in = jnp.einsum("td,te->de", normed_ffn, grad_gate_up, preferred_element_type=jnp.float32)
    grad_norm_ffn = jnp.einsum(
        "te,de->td", grad_gate_up, in_weight, preferred_element_type=jnp.float32
    )
    grad_gain_ffn = jnp.sum(grad_norm_ffn * standard_two, axis=0)
    grad_after = grad_final + norm_back(
        grad_norm_ffn, standard_two, inverse_two, gain_two.astype(jnp.float32)
    )
    ffn_members = (grad_gain_ffn, grad_in, grad_down)
    owned_gain_ffn, owned_in, owned_down = (
        lax.psum_scatter(ffn_members[0], "shard", scatter_dimension=0, tiled=True),
        lax.psum_scatter(ffn_members[1], "shard", scatter_dimension=0, tiled=True),
        lax.psum_scatter(ffn_members[2], "shard", scatter_dimension=0, tiled=True),
    )
    grad_branch = grad_after.astype(jnp.bfloat16)
    grad_out = jnp.einsum("td,te->de", attended, grad_branch, preferred_element_type=jnp.float32)
    grad_attended = jnp.einsum(
        "te,de->td", grad_branch, out_weight, preferred_element_type=jnp.float32
    ).astype(jnp.bfloat16)
    grad_query, grad_key, grad_value = attend_backward(
        queries, keys, values, grad_attended, log_totals
    )
    grad_query = grad_query * cosine + rotate_back(grad_query * sine)
    grad_key = grad_key * cosine + rotate_back(grad_key * sine)
    grad_projected = jnp.stack([grad_query, grad_key, grad_value], axis=1)
    grad_projected = grad_projected.reshape(count_tok, 3 * D).astype(jnp.bfloat16)
    grad_qkv = jnp.einsum(
        "td,te->de", normed_attn, grad_projected, preferred_element_type=jnp.float32
    )
    grad_norm_attn = jnp.einsum(
        "te,de->td", grad_projected, joint_weight, preferred_element_type=jnp.float32
    )
    grad_gain_attn = jnp.sum(grad_norm_attn * standard_one, axis=0)
    input_grad = grad_after + norm_back(
        grad_norm_attn, standard_one, inverse_one, gain_one.astype(jnp.float32)
    )
    attn_members = (grad_gain_attn, grad_qkv, grad_out)
    owned_gain_attn, owned_qkv, owned_out = (
        lax.psum_scatter(attn_members[0], "shard", scatter_dimension=0, tiled=True),
        lax.psum_scatter(attn_members[1], "shard", scatter_dimension=0, tiled=True),
        lax.psum_scatter(attn_members[2], "shard", scatter_dimension=0, tiled=True),
    )
    summed = (
        lax.psum(owned_gain_attn.astype(jnp.bfloat16), "replica").astype(jnp.float32),
        lax.psum(owned_qkv.astype(jnp.bfloat16), "replica").astype(jnp.float32),
        lax.psum(owned_out.astype(jnp.bfloat16), "replica").astype(jnp.float32),
        lax.psum(owned_gain_ffn.astype(jnp.bfloat16), "replica").astype(jnp.float32),
        lax.psum(owned_in.astype(jnp.bfloat16), "replica").astype(jnp.float32),
        lax.psum(owned_down.astype(jnp.bfloat16), "replica").astype(jnp.float32),
    )
    return (
        output,
        input_grad.astype(jnp.bfloat16),
        summed[0],
        summed[1],
        summed[2],
        summed[3],
        summed[4],
        summed[5],
    )


def solution(mesh):
    return jax.shard_map(
        body,
        mesh=mesh,
        in_specs=(
            P(("replica", "shard"), None),
            P("shard"),
            P("shard", None),
            P("shard", None),
            P("shard"),
            P("shard", None),
            P("shard", None),
            P(("replica", "shard"), None),
        ),
        out_specs=(
            P(("replica", "shard"), None),
            P(("replica", "shard"), None),
            P("shard"),
            P("shard", None),
            P("shard", None),
            P("shard"),
            P("shard", None),
            P("shard", None),
        ),
        check_vma=False,
    )
```

profile of v0, /device:TPU:0, one launch (start us, length us, event | category | flops | bytes accessed | tf_op | source)
XLA Modules:
  0.0 722.2 jit_solution(9472683614992483625)
XLA Ops:
  14.4 23.5 %all-reduce.13 = (bf16[768]{0:T(1024)(128)(2,1)S(1)}, bf16[768]{0:T(1024)(128)(2,1)S(1)}) all-reduce(bf16[768]{0:T(1024)(128)(2,1)S(1)} %dynamic-update-slice, bf16[768]{0:T(1024)(128)(2,1)S(1)} %dynamic-update-slice.1), channel_id=1, replica_groups=mesh['replica'=4,'shard'=8] {'shard'}, use_global_device_ids=true, to_apply=%add.8 | all-reduce | flops 1536 | bytes 6144
  39.1 4.4 fusion.101
  46.5 31.9 %all-gather.5.cloned.1.call-done = bf16[768,2304]{1,0:T(8,128)(2,1)} async-done(((bf16[96,2304]{1,0:T(8,128)(2,1)}), bf16[768,2304]{1,0:T(8,128)(2,1)}) %all-gather.5.cloned.1.call-update) | async-done | bytes 3538960 | tf_op jit(solution)/shard_map/all_gather | solution.py:187
  78.4 6.0 fusion.96
  84.4 4.2 slice_bitcast_fusion
  112.8 5.6 squeeze.70
  118.4 4.7 fusion.90
  133.8 4.4 concatenate.87
  143.6 61.0 %while.30 = (s32[]{:T(128)}, bf16[6,512,4,64]{1,3,2,0:T(8,128)(2,1)}, f32[6,4,512]{2,1,0:T(4,128)}, bf16[6,640,4,64]{1,3,2,0:T(8,128)(2,1)}, s32[6]{0:T(128)S(1)...) while((s32[]{:T(128)}, ...), condition=%wide.region_5.6_spmd, body=%wide.region_2.5_spmd.sunk | while | flops 352716416 | bytes 18297728 | solution.py:134
  214.7 10.7 %fusion.110 = f32[1024,2304]{1,0:T(8,128)} fusion(bf16[768,2304]{1,0:T(8,128)(2,1)} %all-gather.9.cloned.1.call-done, f32[1024,768]{0,1:T(8,128)} %copy-done.4, f32[768]{0:T(1024)S(1)} %convert_element_type.164, f32[1024]{0:T(1024)S(1)} %add_rsqrt_fusion, f32[1024]{0:T(1024)S(1)} %broadcast_multiply_fusion.7), kind=kOutput, calls=%fused_computation.187 | convolution fusion | flops 3627024384 | bytes 16133120 | tf_op jit(solution)/shard_map/dot_general | solution.py:210
  225.4 7.5 %all-gather.11.cloned.1.call-done = bf16[1152,768]{1,0:T(8,128)(2,1)} async-done(((bf16[144,768]{1,0:T(8,128)(2,1)}), bf16[1152,768]{1,0:T(8,128)(2,1)}) %all-gather.11.cloned.1.call-update) | async-done | bytes 1769488 | tf_op jit(solution)/shard_map/all_gather | solution.py:193
  232.8 9.2 %fusion.61 = (bf16[1024,1152]{1,0:T(8,128)(2,1)S(1)}, bf16[1024,1152]{1,0:T(8,128)(2,1)S(1)}, bf16[1024,1152]{1,0:T(8,128)(2,1)}) fusion(f32[1024,2304]{1,0:T(8,128)} %fusion.110, bf16[1024,768]{1,0:T(8,128)(2,1)S(1)} %copy-done.20, bf16[1152,768]{1,0:T(8,128)(2,1)} %all-gather.11.cloned.1.call-done), kind=kOutput, calls=%fused_computation.78 | convolution fusion | flops 1830813696 | bytes 19857408 | tf_op jit(solution)/shard_map/td,fd->tf/dot_general | solution.py:230
  242.1 4.9 multiply_reduce_fusion.1
  252.6 5.5 fusion.113
  259.5 4.5 convolution_convert_fusion
  270.5 9.3 %fusion.83 = f32[768,2304]{1,0:T(8,128)} fusion(bf16[1024,1152]{1,0:T(8,128)(2,1)} %copy-done.36, bf16[1024,1152]{1,0:T(8,128)(2,1)} %copy-done.35, f32[1024,768]{0,1:T(8,128)S(1)} %copy-done.6, f32[768]{0:T(1024)S(1)} %convert_element_type.164, f32[1024]{0:T(1024)S(1)} %add_rsqrt_fusion, f32[1024]{0:T(1024)S(1)} %broadcast_multiply_fusion.7), kind=kOutput, calls=%fused_computation.123 | convolution fusion | flops 3636461568 | bytes 14953472 | tf_op jit(solution)/shard_map/td,te->de/dot_general | solution.py:235
  279.8 95.7 %while.31 = (s32[]{:T(128)}, f32[6,512,4,64]{1,3,2,0:T(8,128)}, f32[6,640,4,64]{1,3,2,0:T(8,128)}, f32[6,640,4,64]{1,3,2,0:T(8,128)}, bf16[6,640,4,64]{1,3,2,0:T...) while((s32[]{:T(128)}, f32[6,512,4,64]{1,3,2,0:T(8,128)}, ...), condition=%wide.region_12.13_spmd, body=%wide.region_10.12_spmd.sunk | while | flops 860128896 | bytes 44572060 | solution.py:174
  375.6 5.2 copy.70
  394.9 5.2 copy.71
  406.9 4.3 reshape.527
  411.2 5.6 reshape.526
  420.8 5.6 reshape.532
  426.4 6.0 reshape.531
  432.5 4.1 fusion.86
  445.9 6.2 fusion.94
  452.8 9.3 %fusion.74 = (f32[768]{0:T(1024)S(1)}, f32[1024]{0:T(1024)S(1)}, f32[1024]{0:T(1024)S(1)}, f32[1024,768]{0,1:T(8,128)}) fusion(bf16[1024,768]{0,1:T(8,128)(2,1)S(1)} %copy-done.2, f32[1024]{0:T(1024)S(1)} %copy-done.26, f32[1024]{0:T(1024)S(1)} %copy-done.24, f32[768]{0:T(1024)S(1)} %copy-done.28, bf16[768,2304]{1,0:T(8,128)(2,1)} %all-gather.5.cloned.1.call-done, ...), kind=kOutput, calls=%fused_computation.97 | convolution fusion | flops 3630953728 | bytes 12998656 | tf_op jit(solution)/shard_map/te,de->td/dot_general | solution.py:264
  462.1 20.3 %all-reduce.12 = (bf16[768]{0:T(1024)(128)(2,1)S(1)}, bf16[768]{0:T(1024)(128)(2,1)S(1)}) all-reduce(f32[768]{0:T(1024)S(1)} %get-tuple-element.264, f32[768]{0:T(1024)S(1)} %copy-done.29), channel_id=2, replica_groups=mesh['replica'=4,'shard'=8] {'shard'}, use_global_device_ids=true, to_apply=%region_16.17.clone | all-reduce | flops 1536 | bytes 9216
  482.6 6.2 all-reduce.14
  498.8 36.7 %reduce-scatter.9.cloned.1.call-done = f32[96,2304]{1,0:T(8,128)} async-done(((f32[768,2304]{1,0:T(8,128)}), f32[96,2304]{1,0:T(8,128)}) %reduce-scatter.9.cloned.1.call-update) | async-done | bytes 884752 | tf_op jit(solution)/shard_map/reduce_scatter | solution.py:246
  537.5 130.3 %reduce-scatter.5.cloned.1.call-done = f32[96,2304]{1,0:T(8,128)} async-done(((f32[768,2304]{1,0:T(8,128)}), f32[96,2304]{1,0:T(8,128)}) %reduce-scatter.5.cloned.1.call-update) | async-done | bytes 884752 | tf_op jit(solution)/shard_map/reduce_scatter | solution.py:274
  669.8 5.6 add_convert_fusion
  678.0 31.1 %all-reduce.18.cloned.1.call-done = (bf16[96,2304]{1,0:T(8,128)(2,1)}, bf16[96,768]{1,0:T(8,128)(2,1)}, bf16[96,2304]{1,0:T(8,128)(2,1)}, bf16[144,768]{1,0:T(8,128)(2,1)}) async-done(((bf16[96,2304]{1,0:T(8,128)(2,1)}, bf16[96,768]{1,0:T(8,128)(2,1)}, bf16[96,2304]{1,0:T(8,128)(2,1)}, bf16[144,768]{1,0:T(8,128)(2,1)}), (bf16[96,2304]{1,0:T(8,128)(2,1)}, bf16[96,768]{1,0:T(8,128)(2,1)}, ...) | async-done | bytes 1253392 | tf_op jit(solution)/shard_map/psum | solution.py:279
  (311 shorter events, 279.9 us)
Async XLA Ops:
  7.2 71.2 %all-gather.5.cloned.1.call-start = ((), (), s32[]{:S(2)}) async-start(), calls=%async_computation.4 | async-start | bytes 3981312 | tf_op jit(solution)/shard_map/all_gather | solution.py:187
  7.9 201.3 %all-gather.7.cloned.1.call-start = ((), (), s32[]{:S(2)}) async-start(), calls=%async_computation.5 | async-start | bytes 1327104 | tf_op jit(solution)/shard_map/all_gather | solution.py:188
  8.6 206.0 %all-gather.9.cloned.1.call-start = ((), (), s32[]{:S(2)}) async-start(), calls=%async_computation.6 | async-start | bytes 3981312 | tf_op jit(solution)/shard_map/all_gather | solution.py:192
  9.4 223.4 %all-gather.11.cloned.1.call-start = ((), (), s32[]{:S(2)}) async-start(), calls=%async_computation.7 | async-start | bytes 1990656 | tf_op jit(solution)/shard_map/all_gather | solution.py:193
  10.0 485.3 %reduce-scatter.7.cloned.1.call-start = ((), (), s32[]{:S(2)}) async-start(), calls=%async_computation.9 | async-start | bytes 2654208 | tf_op jit(solution)/shard_map/reduce_scatter | solution.py:275
  10.1 3.9 copy-start.33
  10.1 4.1 copy-start.34
  11.9 197.4 %copy-start.1 = (bf16[1024,768]{0,1:T(8,128)(2,1)}, bf16[1024,768]{0,1:T(8,128)(2,1)S(1)}, u32[]{:S(2)}) copy-start(bf16[1024,768]{0,1:T(8,128)(2,1)S(1)} %copy.59) | copy-start | bytes 4718596
  12.1 66.2 %copy-start.23 = (f32[1024]{0:T(1024)}, f32[1024]{0:T(1024)S(1)}, u32[]{:S(2)}) copy-start(f32[1024]{0:T(1024)S(1)} %broadcast_multiply_fusion.8) | copy-start | bytes 12292
  12.6 71.7 %copy-start.25 = (f32[1024]{0:T(1024)}, f32[1024]{0:T(1024)S(1)}, u32[]{:S(2)}) copy-start(f32[1024]{0:T(1024)S(1)} %add_rsqrt_fusion.1) | copy-start | bytes 12292
  37.9 46.5 %copy-start.27 = (f32[768]{0:T(1024)}, f32[768]{0:T(1024)S(1)}, u32[]{:S(2)}) copy-start(f32[768]{0:T(1024)S(1)} %convert_element_type.157) | copy-start | bytes 9220
  39.0 51.3 %copy-start.16 = (f32[1024,64]{0,1:T(8,128)}, f32[1024,64]{0,1:T(8,128)S(1)}, u32[]{:S(2)}) copy-start(f32[1024,64]{0,1:T(8,128)S(1)} %get-tuple-element.338) | copy-start | bytes 786436
  39.0 51.3 %copy-start.18 = (f32[1024,64]{0,1:T(8,128)}, f32[1024,64]{0,1:T(8,128)S(1)}, u32[]{:S(2)}) copy-start(f32[1024,64]{0,1:T(8,128)S(1)} %get-tuple-element.339) | copy-start | bytes 786436
  100.0 4.1 copy-start.9
  214.7 18.2 %copy-start.20 = (bf16[1024,768]{1,0:T(8,128)(2,1)S(1)}, bf16[1024,768]{1,0:T(8,128)(2,1)}, u32[]{:S(2)}) copy-start(bf16[1024,768]{1,0:T(8,128)(2,1)} %param.19) | copy-start | bytes 4718596
  232.8 9.2 %copy-start.5 = (f32[1024,768]{0,1:T(8,128)S(1)}, f32[1024,768]{0,1:T(8,128)}, u32[]{:S(2)}) copy-start(f32[1024,768]{0,1:T(8,128)} %copy-done.4) | copy-start | bytes 9437188
  232.8 9.2 %copy-start.31 = (bf16[768,2304]{1,0:T(8,128)(2,1)S(1)}, bf16[768,2304]{1,0:T(8,128)(2,1)}, u32[]{:S(2)}) copy-start(bf16[768,2304]{1,0:T(8,128)(2,1)} %all-gather.9.cloned.1.call-done) | copy-start | bytes 10616836
  242.0 4.9 copy-start.35
  242.0 4.9 copy-start.36
  242.1 4.9 copy-start.11
  252.6 244.5 %reduce-scatter.11.cloned.1.call-start = ((), (), s32[]{:S(2)}) async-start(), calls=%async_computation.11 | async-start | bytes 3981312 | tf_op jit(solution)/shard_map/reduce_scatter | solution.py:247
  258.1 277.4 %reduce-scatter.9.cloned.1.call-start = ((), (), s32[]{:S(2)}) async-start(), calls=%async_computation.10 | async-start | bytes 7962624 | tf_op jit(solution)/shard_map/reduce_scatter | solution.py:246
  279.8 388.0 %reduce-scatter.5.cloned.1.call-start = ((), (), s32[]{:S(2)}) async-start(), calls=%async_computation.8 | async-start | bytes 7962624 | tf_op jit(solution)/shard_map/reduce_scatter | solution.py:274
  381.9 2.8 copy-start.14
  401.2 2.8 copy-start.15
  432.5 4.1 copy-start
  432.5 4.5 copy-start.10
  432.5 4.5 copy-start.19
  452.2 256.9 %all-reduce.18.cloned.1.call-start = ((), (), s32[]{:S(2)}) async-start(), calls=%async_computation.12 | async-start | bytes 2506752 | tf_op jit(solution)/shard_map/psum | solution.py:279
  452.8 9.3 %copy-start.29 = (f32[768]{0:T(1024)S(1)}, f32[768]{0:T(1024)}, u32[]{:S(2)}) copy-start(f32[768]{0:T(1024)} %get-tuple-element.262) | copy-start | bytes 9220
  495.3 174.5 %copy-start.7 = (f32[1024,768]{0,1:T(8,128)S(1)}, f32[1024,768]{0,1:T(8,128)}, u32[]{:S(2)}) copy-start(f32[1024,768]{0,1:T(8,128)} %copy-done.4) | copy-start | bytes 9437188
  709.0 5.7 copy-start.22
  (15 other events, 33.8 us)
Sparse Core Ops, SparseCore 0:
  10.2 68.1 all-gather.4
  80.5 39.5 all-gather.6
  122.3 63.9 all-gather.8
  188.3 44.4 all-gather.10
  252.7 68.0 reduce-scatter.6
  324.2 78.1 reduce-scatter.10
  406.1 129.3 reduce-scatter.8
  539.6 128.0 reduce-scatter.4
  671.0 38.0 all-reduce.17
where the time goes:
time: 734 us; the launch traced here: 722 us
  waiting for transfers between devices  240 us (33%)
  matrix products  179 us (24%)
  local copies, waits for them, and re-layouts  142 us (19%)
  other arithmetic  86 us (12%)
  blocking collectives  50 us (7%)
  between operations  16 us (2%)
  loops' own time  8.62 us (1%)
    reduce_scatter x1, waiting for transfers between devices, body(): lax.psum_scatter(attn_members[1], 'shard', scatter_dimension=0, tiled=True)  130 us
    unnamed x2, blocking collectives  43.8 us
    reduce_scatter x1, waiting for transfers between devices, body(): lax.psum_scatter(ffn_members[1], 'shard', scatter_dimension=0, tiled=True)  36.7 us
    all_gather x1, waiting for transfers between devices, body(): lax.all_gather(w_qkv, 'shard', axis=0, tiled=True)  31.9 us
    psum x1, waiting for transfers between devices, body(): lax.psum(owned_qkv.astype(jnp.bfloat16), 'replica').astype(jnp.float32)  31.1 us
    dot_general x12, matrix products, block_scores(): jnp.einsum('qhd,khd->hqk', query_part, key_part, preferred_element_type=j...  24.6 us
    unnamed x86, local copies, waits for them, and re-layouts  21.1 us
    dot_general x6, matrix products, one_block(): jnp.einsum('hqk,khd->qhd', probs, value_part, preferred_element_type=jnp....  20.8 us
  transfers between devices with their start and end apart: 9, of which 5 were waited for; matrix products, arithmetic and copies ran while one was open for 51% of the time, Pallas kernels for 0%

commit v1 on v0

v1 whole, which is shorter than its diff:
```python
import functools

import jax
import jax.numpy as jnp
from jax import lax
from jax.experimental import pallas as pl
from jax.experimental.pallas import tpu as pltpu
from jax.sharding import PartitionSpec as P

D = 768
HEADS = 12
HEAD_DIM = 64
FF = 1152
WINDOW = 128
LENGTH = 1024
MARGIN = WINDOW // 2
QB = 128
SPAN = QB + 2 * MARGIN
PAIRS = D // 128
SCALE = HEAD_DIM ** (-0.5)
F32 = jnp.float32
BF16 = jnp.bfloat16
EPS = 1e-05
LIMIT = 60 * 1024 * 1024


def dot(a, b):
    return jnp.dot(a, b, preferred_element_type=F32)


def dot_nt(a, b):
    return lax.dot_general(a, b, (((1,), (1,)), ((), ())), preferred_element_type=F32)


def dot_tn(a, b):
    return lax.dot_general(a, b, (((0,), (0,)), ((), ())), preferred_element_type=F32)


def normalize(values):
    centre = values - jnp.mean(values, axis=-1, keepdims=True)
    inverse = lax.rsqrt(jnp.mean(centre * centre, axis=-1, keepdims=True) + EPS)
    return centre * inverse, inverse


def norm_back(grad_norm, standard, inverse, gain):
    scaled = grad_norm * gain
    return inverse * (
        scaled
        - jnp.mean(scaled, axis=-1, keepdims=True)
        - standard * jnp.mean(scaled * standard, axis=-1, keepdims=True)
    )


def rotary_tables(count):
    half_dim = HEAD_DIM // 2
    freqs = 10000.0 ** (-(jnp.arange(half_dim, dtype=F32) * 2.0) / HEAD_DIM)
    angles = jnp.arange(count, dtype=jnp.int32).astype(F32)[:, None] * freqs[None, :]
    cosine, sine = jnp.cos(angles), jnp.sin(angles)
    return (
        jnp.concatenate([cosine] * 4, axis=1),
        jnp.concatenate([-sine, sine, -sine, sine], axis=1),
    )


def swapped(u):
    lane = lax.broadcasted_iota(jnp.int32, u.shape, 1)
    return jnp.where((lane % 64) < 32, pltpu.roll(u, 96, 1), pltpu.roll(u, 32, 1))


def stack_heads(u):
    first = lax.broadcasted_iota(jnp.int32, u.shape, 1) < HEAD_DIM
    zero = jnp.zeros_like(u)
    return jnp.concatenate([jnp.where(first, u, zero), jnp.where(first, zero, u)], axis=0)


def merge_heads(u):
    top, low = u[:QB], u[QB:]
    first = lax.broadcasted_iota(jnp.int32, top.shape, 1) < HEAD_DIM
    return jnp.where(first, top, low)


def block_place(i):
    q_start = pl.multiple_of(i * QB, QB)
    k_start = pl.multiple_of(jnp.clip(i * QB - MARGIN, 0, LENGTH - SPAN), MARGIN)
    row = lax.broadcasted_iota(jnp.int32, (2 * QB, SPAN), 0)
    col = lax.broadcasted_iota(jnp.int32, (2 * QB, SPAN), 1)
    allowed = jnp.abs(q_start + (row % QB) - (k_start + col)) <= MARGIN
    return q_start, k_start, allowed


def softmax(queries, keys, allowed):
    scores = jnp.where(allowed, dot_nt(queries, keys), -1e30)
    expo = jnp.exp(scores - jnp.max(scores, axis=-1, keepdims=True))
    return expo * (1.0 / jnp.sum(expo, axis=-1, keepdims=True))


def attend_kernel(x_ref, gain_ref, w_ref, cos_ref, sin_ref, q_ref, k_ref, v_ref, att_ref):
    chunk = 256

    @pl.loop(0, LENGTH // chunk)
    def _(c):
        rows = pl.ds(pl.multiple_of(c * chunk, chunk), chunk)
        standard, _ = normalize(x_ref[rows, :].astype(F32))
        normed = (standard * gain_ref[...]).astype(BF16)
        cosine, sine = cos_ref[rows, :], sin_ref[rows, :]
        for part, ref in ((0, q_ref), (1, k_ref)):
            raw = dot(normed, w_ref[:, part * D : (part + 1) * D])
            for g in range(PAIRS):
                u = raw[:, g * 128 : (g + 1) * 128]
                ref[rows, g * 128 : (g + 1) * 128] = (u * cosine + swapped(u) * sine).astype(BF16)
        v_ref[rows, :] = dot(normed, w_ref[:, 2 * D :]).astype(BF16)

    @pl.loop(0, LENGTH // QB)
    def _(i):
        q_start, k_start, allowed = block_place(i)
        for g in range(PAIRS):
            lanes = slice(g * 128, (g + 1) * 128)
            queries = stack_heads(q_ref[pl.ds(q_start, QB), lanes] * SCALE)
            probs = softmax(queries, k_ref[pl.ds(k_start, SPAN), lanes], allowed)
            mixed = dot(probs.astype(BF16), v_ref[pl.ds(k_start, SPAN), lanes])
            att_ref[pl.ds(q_start, QB), lanes] = merge_heads(mixed).astype(BF16)


def column_of(row):
    return jnp.transpose(jnp.broadcast_to(row, (128, D)))


def ffn_kernel(
    x_ref, att_ref, cot_ref, gain_ref, wo_ref, wi_ref, wd_ref,
    out_ref, after_ref, gatt_ref, gout_ref, gin_ref, gdown_ref,
    out_acc, in_acc, down_acc, gain_acc,
):
    step = pl.program_id(0)

    @pl.when(step == 0)
    def _():
        out_acc[...] = jnp.zeros_like(out_acc)
        in_acc[...] = jnp.zeros_like(in_acc)
        down_acc[...] = jnp.zeros_like(down_acc)
        gain_acc[...] = jnp.zeros_like(gain_acc)

    att = att_ref[...]
    cot = cot_ref[...]
    gain = gain_ref[...]
    after = x_ref[...].astype(F32) + dot(att, wo_ref[...])
    standard, inverse = normalize(after)
    normed = (standard * gain).astype(BF16)
    lifted = dot(normed, wi_ref[:, :FF])
    gate = dot(normed, wi_ref[:, FF:])
    grad_act = dot_nt(cot, wd_ref[...])
    cdf = 0.5 * (1.0 + lax.erf(lifted * 0.7071067811865476))
    gelu = lifted * cdf
    activated = (gelu * gate).astype(BF16)
    density = jnp.exp(-0.5 * lifted * lifted) * 0.3989422804014327
    grad_lifted = (grad_act * gate * (cdf + lifted * density)).astype(BF16)
    grad_gate = (grad_act * gelu).astype(BF16)
    out_ref[...] = (after + dot(activated, wd_ref[...])).astype(BF16)
    down_acc[...] += dot_tn(activated, cot)
    in_acc[:, :FF] += dot_tn(normed, grad_lifted)
    in_acc[:, FF:] += dot_tn(normed, grad_gate)
    grad_norm = dot_nt(grad_lifted, wi_ref[:, :FF]) + dot_nt(grad_gate, wi_ref[:, FF:])
    gain_acc[...] += jnp.sum(grad_norm * standard, axis=0, keepdims=True)
    grad_after = cot.astype(F32) + norm_back(grad_norm, standard, inverse, gain)
    after_ref[...] = grad_after
    branch = grad_after.astype(BF16)
    out_acc[...] += dot_tn(att, branch)
    gatt_ref[...] = dot_nt(branch, wo_ref[...]).astype(BF16)

    @pl.when(step == pl.num_programs(0) - 1)
    def _():
        for h in range(2):
            gout_ref[h] = out_acc[:, h * (D // 2) : (h + 1) * (D // 2)].astype(BF16)
            gdown_ref[h] = down_acc[:, h * (D // 2) : (h + 1) * (D // 2)].astype(BF16)
            gin_ref[h, :, :FF] = in_acc[:, h * FF : (h + 1) * FF].astype(BF16)
            gin_ref[h, :, FF:] = column_of(gain_acc[...]).astype(BF16)


def back_kernel(
    q_ref, k_ref, v_ref, gatt_ref, cos_ref, sin_ref, gp_ref, dk_ref, dv_ref
):
    dk_ref[...] = jnp.zeros_like(dk_ref)
    dv_ref[...] = jnp.zeros_like(dv_ref)

    @pl.loop(0, LENGTH // QB)
    def _(i):
        q_start, k_start, allowed = block_place(i)
        q_rows, k_rows = pl.ds(q_start, QB), pl.ds(k_start, SPAN)
        cosine, sine = cos_ref[q_rows, :], sin_ref[q_rows, :]
        for g in range(PAIRS):
            lanes = slice(g * 128, (g + 1) * 128)
            queries = stack_heads(q_ref[q_rows, lanes] * SCALE)
            keys = k_ref[k_rows, lanes]
            grads = stack_heads(gatt_ref[q_rows, lanes])
            probs = softmax(queries, keys, allowed)
            grad_probs = dot_nt(grads, v_ref[k_rows, lanes])
            centre = jnp.sum(grad_probs * probs, axis=-1, keepdims=True)
            grad_scores = (probs * (grad_probs - centre)).astype(BF16)
            u = merge_heads(dot(grad_scores, keys)) * SCALE
            gp_ref[q_rows, lanes] = (u * cosine - swapped(u) * sine).astype(BF16)
            dk_ref[k_rows, lanes] += dot_tn(grad_scores, queries)
            dv_ref[k_rows, lanes] += dot_tn(probs.astype(BF16), grads)

    chunk = 256

    @pl.loop(0, LENGTH // chunk)
    def _(c):
        rows = pl.ds(pl.multiple_of(c * chunk, chunk), chunk)
        cosine, sine = cos_ref[rows, :], sin_ref[rows, :]
        for g in range(PAIRS):
            u = dk_ref[rows, g * 128 : (g + 1) * 128]
            gp_ref[rows, D + g * 128 : D + (g + 1) * 128] = (
                u * cosine - swapped(u) * sine
            ).astype(BF16)
        gp_ref[rows, 2 * D :] = dv_ref[rows, :].astype(BF16)


def last_kernel(
    x_ref, after_ref, gp_ref, gain_ref, w_ref, ig_ref, gq_ref, acc, gain_acc
):
    step = pl.program_id(0)

    @pl.when(step == 0)
    def _():
        acc[...] = jnp.zeros_like(acc)
        gain_acc[...] = jnp.zeros_like(gain_acc)

    gain = gain_ref[...]
    standard, inverse = normalize(x_ref[...].astype(F32))
    normed = (standard * gain).astype(BF16)
    grad_projected = gp_ref[...]
    acc[...] += dot_tn(normed, grad_projected)
    grad_norm = dot_nt(grad_projected, w_ref[...])
    gain_acc[...] += jnp.sum(grad_norm * standard, axis=0, keepdims=True)
    ig_ref[...] = (after_ref[...] + norm_back(grad_norm, standard, inverse, gain)).astype(BF16)

    @pl.when(step == pl.num_programs(0) - 1)
    def _():
        for h in range(2):
            gq_ref[h, :, :FF] = acc[:, h * FF : (h + 1) * FF].astype(BF16)
            gq_ref[h, :, FF:] = column_of(gain_acc[...]).astype(BF16)


def shape(dims, dtype):
    return jax.ShapeDtypeStruct(dims, dtype)


def cost(flops, bytes_accessed):
    return pl.CostEstimate(flops=flops, bytes_accessed=bytes_accessed, transcendentals=0)


PARAMS = pltpu.CompilerParams(vmem_limit_bytes=LIMIT)
WHOLE = pl.BlockSpec(memory_space=pltpu.VMEM)
ROWS = 256


def by_rows(width):
    return pl.BlockSpec((ROWS, width), lambda i: (i, 0))


def fixed(*dims):
    return pl.BlockSpec(dims, lambda i: (0,) * len(dims), pipeline_mode=pl.Buffered(1))


def attend(x, gain, w, cosine, sine):
    t = x.shape[0]
    return pl.pallas_call(
        attend_kernel,
        out_shape=[shape((t, D), BF16)] * 4,
        in_specs=[WHOLE] * 5,
        out_specs=[WHOLE] * 4,
        compiler_params=PARAMS,
        cost_estimate=cost(8_000_000_000, 14_000_000),
        name="attend",
    )(x, gain, w, cosine, sine)


def ffn(x, att, cot, gain, wo, wi, wd):
    t = x.shape[0]
    return pl.pallas_call(
        ffn_kernel,
        grid=(t // ROWS,),
        in_specs=[
            by_rows(D), by_rows(D), by_rows(D), fixed(1, D),
            fixed(D, D), fixed(D, 2 * FF), fixed(FF, D),
        ],
        out_specs=[
            by_rows(D), by_rows(D), by_rows(D),
            fixed(2, D, D // 2), fixed(2, D, FF + 128), fixed(2, FF, D // 2),
        ],
        out_shape=[
            shape((t, D), BF16), shape((t, D), F32), shape((t, D), BF16),
            shape((2, D, D // 2), BF16), shape((2, D, FF + 128), BF16), shape((2, FF, D // 2), BF16),
        ],
        scratch_shapes=[
            pltpu.VMEM((D, D), F32), pltpu.VMEM((D, 2 * FF), F32),
            pltpu.VMEM((FF, D), F32), pltpu.VMEM((1, D), F32),
        ],
        compiler_params=PARAMS,
        cost_estimate=cost(20_000_000_000, 25_000_000),
        name="ffn",
    )(x, att, cot, gain, wo, wi, wd)


def back(q, k, v, gatt, cosine, sine):
    t = q.shape[0]
    return pl.pallas_call(
        back_kernel,
        out_shape=shape((t, 3 * D), BF16),
        in_specs=[WHOLE] * 6,
        out_specs=WHOLE,
        scratch_shapes=[pltpu.VMEM((t, D), F32), pltpu.VMEM((t, D), F32)],
        compiler_params=PARAMS,
        cost_estimate=cost(10_000_000_000, 14_000_000),
        name="back",
    )(q, k, v, gatt, cosine, sine)


def last(x, after, gp, gain, w):
    t = x.shape[0]
    return pl.pallas_call(
        last_kernel,
        grid=(t // ROWS,),
        in_specs=[by_rows(D), by_rows(D), by_rows(3 * D), fixed(1, D), fixed(D, 3 * D)],
        out_specs=[by_rows(D), fixed(2, D, FF + 128)],
        out_shape=[shape((t, D), BF16), shape((2, D, FF + 128), BF16)],
        scratch_shapes=[pltpu.VMEM((D, 3 * D), F32), pltpu.VMEM((1, D), F32)],
        compiler_params=PARAMS,
        cost_estimate=cost(8_000_000_000, 20_000_000),
        name="last",
    )(x, after, gp, gain, w)


def body(copies, tokens, gain_attn, w_qkv, w_out, gain_ffn, w_in, w_down, cotangent):
    core = lax.axis_index("replica") % 2
    to_core = [(r, r ^ 1) for r in range(copies)]
    to_chip = [(r, r ^ 2) for r in range(copies)]

    def in_order(mine, other):
        return jnp.concatenate(
            [jnp.where(core == 0, mine, other), jnp.where(core == 0, other, mine)], axis=1
        )

    def half_of(w):
        width = w.shape[1] // 2
        return lax.dynamic_slice_in_dim(w, core * width, width, 1)

    def gather(w):
        mine = lax.all_gather(w, "shard", axis=0, tiled=True)
        return mine, lax.ppermute(mine, "replica", to_core)

    def reduce_rows(g):
        mine = lax.dynamic_index_in_dim(g, core, 0, keepdims=False)
        theirs = lax.dynamic_index_in_dim(g, 1 - core, 0, keepdims=False)
        theirs = lax.ppermute(theirs, "replica", to_core)
        part = (mine.astype(F32) + theirs.astype(F32)).astype(BF16)
        part = lax.psum_scatter(part, "shard", scatter_dimension=0, tiled=True)
        for perm in () if copies < 4 else (to_chip,):
            across = lax.ppermute(part, "replica", perm)
            part = (part.astype(F32) + across.astype(F32)).astype(BF16)
        other = lax.ppermute(part, "replica", to_core)
        return part.astype(F32), other.astype(F32)

    gains = jnp.stack([gain_attn, gain_ffn], axis=1)
    gains = jnp.pad(gains, ((0, 0), (0, 126)))
    mine, other = gather(jnp.concatenate([half_of(w_qkv), gains], axis=1))
    joint = in_order(mine[:, :FF], other[:, :FF])
    gain_one = mine[:, FF].astype(F32)[None, :]
    gain_two = mine[:, FF + 1].astype(F32)[None, :]
    out_weight = in_order(*gather(half_of(w_out)))
    in_weight = in_order(*gather(half_of(w_in)))
    down_weight = in_order(*gather(half_of(w_down)))

    cosine, sine = rotary_tables(LENGTH)
    q, k, v, att = attend(tokens, gain_one, joint, cosine, sine)
    output, after, gatt, gout, gin, gdown = ffn(
        tokens, att, cotangent, gain_two, out_weight, in_weight, down_weight
    )
    gp = back(q, k, v, gatt, cosine, sine)
    input_grad, gqkv = last(tokens, after, gp, gain_one, joint)

    in_mine, in_other = reduce_rows(gin)
    grad_down = in_order(*reduce_rows(gdown))
    grad_out = in_order(*reduce_rows(gout))
    qkv_mine, qkv_other = reduce_rows(gqkv)
    return (
        output,
        input_grad,
        qkv_mine[:, FF],
        in_order(qkv_mine[:, :FF], qkv_other[:, :FF]),
        grad_out,
        in_mine[:, FF],
        in_order(in_mine[:, :FF], in_other[:, :FF]),
        grad_down,
    )


def solution(mesh):
    return jax.shard_map(
        functools.partial(body, mesh.shape["replica"]),
        mesh=mesh,
        in_specs=(
            P(("replica", "shard"), None),
            P("shard"),
            P("shard", None),
            P("shard", None),
            P("shard"),
            P("shard", None),
            P("shard", None),
            P(("replica", "shard"), None),
        ),
        out_specs=(
            P(("replica", "shard"), None),
            P(("replica", "shard"), None),
            P("shard"),
            P("shard", None),
            P("shard", None),
            P("shard"),
            P("shard", None),
            P("shard", None),
        ),
        check_vma=False,
    )
```

time: 734 us -> 471 us (0.64); the launches traced: 722 us -> 470 us
  matrix products: 179 us -> 0 us
  local copies, waits for them, and re-layouts: 142 us -> 14.3 us
  Pallas kernels: 0 us -> 108 us
  other arithmetic: 86 us -> 30.1 us
  blocking collectives: 50 us -> 67.6 us
  waiting for transfers between devices: 240 us -> 227 us
  loops' own time: 8.62 us -> 0 us
  starting transfers between devices: 0.36 us -> 8.92 us
    dot_general x54 -> x0, matrix products: 179 us -> none  [the longest x12 24.6 us: block_scores(): jnp.einsum('qhd,khd->hqk', query_part, key_part, preferred_element_type=j...]
    pallas_call x0 -> x4, Pallas kernels: none -> 108 us  [the longest x1 35.8 us: ffn(): pl.pallas_call(ffn_kernel, grid=(t // ROWS,), in_specs=[by_rows(D), by_ro...]
    all_gather x0 -> x2, blocking collectives: none -> 67.6 us  [gather(): mine = lax.all_gather(w, 'shard', axis=0, tiled=True)]
    unnamed x2 -> x0, blocking collectives: 43.8 us -> none
    reshape x9 -> x0, local copies, waits for them, and re-layouts: 34.9 us -> none  [the longest x2 11.6 us: unwindow(): shaped[:, :, :block_rows].reshape(seq_count, LENGTH, HEADS, HEAD_DIM)]
    psum x1 -> x0, waiting for transfers between devices: 31.1 us -> none  [body(): lax.psum(owned_qkv.astype(jnp.bfloat16), 'replica').astype(jnp.float32)]
    unnamed x86 -> x18, local copies, waits for them, and re-layouts: 21.1 us -> 1.77 us
    ppermute x0 -> x16, waiting for transfers between devices: none -> 16.7 us  [the longest x4 10.5 us: reduce_rows(): across = lax.ppermute(part, 'replica', perm)]
  transfers between devices with their start and end apart: 9 -> 22, of which waited for: 5 -> 9; matrix products, arithmetic and copies ran while one was open for 51% -> 8% of each run, Pallas kernels for 0% -> 11%
where the time goes in v1:
time: 471 us; the launch traced here: 470 us
  waiting for transfers between devices  227 us (48%)
  Pallas kernels  108 us (23%)
  blocking collectives  67.6 us (14%)
  other arithmetic  30.1 us (6%)
  between operations  14.4 us (3%)
  local copies, waits for them, and re-layouts  14.3 us (3%)
  starting transfers between devices  8.92 us (2%)
    reduce_scatter x4, waiting for transfers between devices, reduce_rows(): part = lax.psum_scatter(part, 'shard', scatter_dimension=0, tiled=True)  179 us
    all_gather x2, blocking collectives, gather(): mine = lax.all_gather(w, 'shard', axis=0, tiled=True)  67.6 us
    pallas_call x1, Pallas kernels, ffn(): pl.pallas_call(ffn_kernel, grid=(t // ROWS,), in_specs=[by_rows(D), by_ro...  35.8 us
    pallas_call x1, Pallas kernels, back(): pl.pallas_call(back_kernel, out_shape=shape((t, 3 * D), BF16), in_specs=[...  35.6 us
    all_gather x2, waiting for transfers between devices, gather(): mine = lax.all_gather(w, 'shard', axis=0, tiled=True)  30.8 us
    pallas_call x1, Pallas kernels, attend(): pl.pallas_call(attend_kernel, out_shape=[shape((t, D), BF16)] * 4, in_spe...  20.5 us
    pallas_call x1, Pallas kernels, last(): pl.pallas_call(last_kernel, grid=(t // ROWS,), in_specs=[by_rows(D), by_r...  16.2 us
    ppermute x4, waiting for transfers between devices, reduce_rows(): across = lax.ppermute(part, 'replica', perm)  10.5 us
  transfers between devices with their start and end apart: 22, of which 9 were waited for; matrix products, arithmetic and copies ran while one was open for 8% of the time, Pallas kernels for 11%

profile of v1, /device:TPU:0, one launch (start us, length us, event | category | flops | bytes accessed | tf_op | source)
XLA Modules:
  0.0 470.1 jit_solution(4207864437471990986)
XLA Ops:
  11.6 35.3 %all_gather.15 = bf16[1152,384]{1,0:T(8,128)(2,1)S(1)} all-gather(bf16[144,384]{1,0:T(8,128)(2,1)S(1)} %constant_dynamic-slice_fusion), channel_id=1, replica_groups=mesh['replica'=4,'shard'=8] {'shard'}, dimensions={0}, use_global_device_ids=true | all-gather | bytes 995328 | tf_op jit(solution)/shard_map/all_gather | solution.py:348
  46.8 32.4 %all_gather.13 = bf16[768,384]{1,0:T(8,128)(2,1)S(1)} all-gather(bf16[96,384]{1,0:T(8,128)(2,1)S(1)} %constant_dynamic-slice_fusion.2), channel_id=1, replica_groups=mesh['replica'=4,'shard'=8] {'shard'}, dimensions={0}, use_global_device_ids=true | all-gather | bytes 663552 | tf_op jit(solution)/shard_map/all_gather | solution.py:348
  79.9 1.9 fusion.6
  81.8 1.9 pad_maximum_fusion.6
  84.9 30.8 %all-gather.3.cloned.1.call-done = bf16[768,1280]{1,0:T(8,128)(2,1)} async-done(((bf16[96,1280]{1,0:T(8,128)(2,1)}), bf16[768,1280]{1,0:T(8,128)(2,1)}) %all-gather.3.cloned.1.call-update) | async-done | bytes 1966096 | tf_op jit(solution)/shard_map/all_gather | solution.py:348
  115.9 1.4 pad_maximum_fusion.2.wd_ref
  119.5 1.8 broadcast_select_fusion.1
  121.3 2.0 pad_maximum_fusion.1.wi_ref
  123.7 2.0 pad_maximum_fusion.w_ref
  125.7 20.5 %attend.1 = (bf16[1024,768]{1,0:T(8,128)(2,1)}, bf16[1024,768]{1,0:T(8,128)(2,1)}, bf16[1024,768]{1,0:T(8,128)(2,1)}, bf16[1024,768]{1,0:T(8,128)(2,1)}) custom-call(bf16[1024,768]{1,0:T(8,128)(2,1)} %x_ref.5, f32[1,768]{1,0:T(1,128)} %reshape.59.gain_ref, bf16[768,2304]{1,0:T(8,128)(2,1)} %pad_maximum_fusion.w_ref, f32[1024,128]{1,0:T(8,128)} %get-tuple-element.57.cos_ref, ...), custom_call_target="tpu_custom_call" | custom-call | flops 8000000000 | bytes 14000000 | tf_op jit(solution)/shard_map/attend/pallas_call | solution.py:266
  146.2 35.8 %ffn.1 = (bf16[1024,768]{1,0:T(8,128)(2,1)}, f32[1024,768]{1,0:T(8,128)}, bf16[1024,768]{1,0:T(8,128)(2,1)}, bf16[2,768,384]{2,1,0:T(8,128)(2,1)}, bf16[2,768,12...) custom-call(bf16[1024,768]{1,0:T(8,128)(2,1)} %x_ref.5, bf16[1024,768]{1,0:T(8,128)(2,1)} %get-tuple-element.20.att_ref, ...), custom_call_target="tpu_custom_call" | custom-call | flops 20000000000 | bytes 25000000 | tf_op jit(solution)/shard_map/ffn/pallas_call | solution.py:279
  182.0 1.2 dynamic-slice_bitcast_fusion.3
  183.8 2.2 dynamic-slice_bitcast_fusion.2
  186.0 2.0 fusion.3
  188.1 3.1 dynamic-slice_bitcast_fusion
  192.9 2.6 collective-permute-done.10
  195.5 3.3 fusion
  199.0 35.6 %back.1.gp_ref = bf16[1024,2304]{1,0:T(8,128)(2,1)} custom-call(bf16[1024,768]{1,0:T(8,128)(2,1)} %get-tuple-element.23.q_ref, bf16[1024,768]{1,0:T(8,128)(2,1)} %get-tuple-element.24.k_ref, bf16[1024,768]{1,0:T(8,128)(2,1)} %get-tuple-element.25.v_ref, bf16[1024,768]{1,0:T(8,128)(2,1)} %get-tuple-element.26.gatt_ref, ...), custom_call_target="tpu_custom_call" | custom-call | flops 10000000000 | bytes 14000000 | tf_op jit(solution)/shard_map/back/pallas_call | solution.py:306
  234.6 16.2 %last.1 = (bf16[1024,768]{1,0:T(8,128)(2,1)}, bf16[2,768,1280]{2,1,0:T(8,128)(2,1)}) custom-call(bf16[1024,768]{1,0:T(8,128)(2,1)} %x_ref.5, f32[1024,768]{1,0:T(8,128)} %get-tuple-element.22.after_ref, bf16[1024,2304]{1,0:T(8,128)(2,1)} %back.1.gp_ref, f32[1,768]{1,0:T(1,128)} %reshape.59.gain_ref, bf16[768,2304]{1,0:T(8,128)(2,1)} %pad_maximum_fusion.w_ref), custom_call_target="tpu_custom_call" | custom-call | flops 8000000000 | bytes 20000000 | tf_op jit(solution)/shard_map/last/pallas_call | solution.py:320
  250.9 1.8 dynamic-slice_bitcast_fusion.1
  253.2 3.6 collective-permute-done.4
  256.8 1.8 fusion.1
  258.6 1.5 collective-permute-start.8
  260.2 3.3 collective-permute-done.8
  264.4 49.6 %reduce-scatter.11.cloned.1.call-done = bf16[144,384]{1,0:T(8,128)(2,1)} async-done(((bf16[1152,384]{1,0:T(8,128)(2,1)}), bf16[144,384]{1,0:T(8,128)(2,1)}) %reduce-scatter.11.cloned.1.call-update) | async-done | bytes 110608 | tf_op jit(solution)/shard_map/reduce_scatter | solution.py:356
  314.1 1.5 collective-permute-start.14
  315.6 3.5 collective-permute-done.14
  320.8 62.7 %reduce-scatter.9.cloned.1.call-done = bf16[96,1280]{1,0:T(8,128)(2,1)} async-done(((bf16[768,1280]{1,0:T(8,128)(2,1)}), bf16[96,1280]{1,0:T(8,128)(2,1)}) %reduce-scatter.9.cloned.1.call-update) | async-done | bytes 245776 | tf_op jit(solution)/shard_map/reduce_scatter | solution.py:356
  383.5 1.5 collective-permute-start.11
  385.8 66.6 %reduce-scatter.5.cloned.1.call-done = bf16[96,1280]{1,0:T(8,128)(2,1)} async-done(((bf16[768,1280]{1,0:T(8,128)(2,1)}), bf16[96,1280]{1,0:T(8,128)(2,1)}) %reduce-scatter.5.cloned.1.call-update) | async-done | bytes 245776 | tf_op jit(solution)/shard_map/reduce_scatter | solution.py:356
  452.5 1.6 collective-permute-start.5
  455.1 3.7 collective-permute-done.5
  (86 shorter events, 21.1 us)
Async XLA Ops:
  7.2 1.0 copy-start
  7.2 4.4 copy-start.7
  7.2 39.6 %copy-start.8 = (bf16[96,768]{1,0:T(8,128)(2,1)S(1)}, bf16[96,768]{1,0:T(8,128)(2,1)}, u32[]{:S(2)}) copy-start(bf16[96,768]{1,0:T(8,128)(2,1)} %param.11) | copy-start | bytes 442372
  7.2 72.1 %all-gather.5.cloned.1.call-start = ((), (), s32[]{:S(2)}) async-start(), calls=%async_computation.5 | async-start | bytes 1990656 | tf_op jit(solution)/shard_map/all_gather | solution.py:348
  8.9 106.8 %all-gather.3.cloned.1.call-start = ((), (), s32[]{:S(2)}) async-start(), calls=%async_computation.4 | async-start | bytes 2211840 | tf_op jit(solution)/shard_map/all_gather | solution.py:348
  11.5 247.1 %reduce-scatter.7.cloned.1.call-start = ((), (), s32[]{:S(2)}) async-start(), calls=%async_computation.7 | async-start | bytes 663552 | tf_op jit(solution)/shard_map/reduce_scatter | solution.py:356
  46.8 68.9 %collective-permute-start.3 = (bf16[1152,384]{1,0:T(8,128)(2,1)S(1)}, bf16[1152,384]{1,0:T(8,128)(2,1)S(1)}, u32[]{:S(2)}, u32[]{:S(2)}) collective-permute-start(bf16[1152,384]{1,0:T(8,128)(2,1)S(1)} %all_gather.15), channel_id=1, source_target_pairs={{0,8},{8,0},{16,24},{24,16},{1,9},{9,1},{17,25},{25,17},{2,10},{10... | collective-permute-start | bytes 2654216 | tf_op jit(solution)/shard_map/ppermute | solution.py:349
  79.2 4.4 collective-permute-start.1
  79.3 40.2 %collective-permute-start.2 = (bf16[768,1152]{1,0:T(8,128)(2,1)}, bf16[768,1152]{1,0:T(8,128)(2,1)}, u32[]{:S(2)}, u32[]{:S(2)}) collective-permute-start(bf16[768,1152]{1,0:T(8,128)(2,1)} %all-gather.5.cloned.1.call-done), channel_id=1, source_target_pairs={{0,8},{8,0},{16,24},{24,16},{1,9},{9,1},{17,25},{25,17},{2,10},{10... | collective-permute-start | bytes 5308424 | tf_op jit(solution)/shard_map/ppermute | solution.py:349
  115.7 7.6 %collective-permute-start = (bf16[768,1280]{1,0:T(8,128)(2,1)}, bf16[768,1280]{1,0:T(8,128)(2,1)S(1)}, u32[]{:S(2)}, u32[]{:S(2)}) collective-permute-start(bf16[768,1280]{1,0:T(8,128)(2,1)} %all-gather.3.cloned.1.call-done), channel_id=1, source_target_pairs={{0,8},{8,0},{16,24},{24,16},{1,9},{9,1},{17,25},{25,17},{2,10},{10... | collective-permute-start | bytes 5898248 | tf_op jit(solution)/shard_map/ppermute | solution.py:349
  115.9 2.2 copy-start.3
  115.9 3.6 copy-start.4
  182.0 4.0 copy-start.6
  183.2 2.8 collective-permute-start.7
  185.9 5.7 %collective-permute-start.13 = (bf16[1152,384]{1,0:T(8,128)(2,1)}, bf16[1152,384]{1,0:T(8,128)(2,1)S(1)}, u32[]{:S(2)}, u32[]{:S(2)}) collective-permute-start(bf16[1152,384]{1,0:T(8,128)(2,1)} %dynamic-slice_bitcast_fusion.2), channel_id=1, source_target_pairs={{0,8},{8,0},{16,24},{24,16},{1,9},{9,1},{17,25},{25,17},{2,10},{10... | collective-permute-start | bytes 2654216 | tf_op jit(solution)/shard_map/ppermute | solution.py:354
  188.0 126.1 %reduce-scatter.11.cloned.1.call-start = ((), (), s32[]{:S(2)}) async-start(), calls=%async_computation.9 | async-start | bytes 995328 | tf_op jit(solution)/shard_map/reduce_scatter | solution.py:356
  188.1 3.6 copy-start.5
  191.2 4.3 collective-permute-start.10
  192.8 190.7 %reduce-scatter.9.cloned.1.call-start = ((), (), s32[]{:S(2)}) async-start(), calls=%async_computation.8 | async-start | bytes 2211840 | tf_op jit(solution)/shard_map/reduce_scatter | solution.py:356
  198.7 253.7 %reduce-scatter.5.cloned.1.call-start = ((), (), s32[]{:S(2)}) async-start(), calls=%async_computation.6 | async-start | bytes 2211840 | tf_op jit(solution)/shard_map/reduce_scatter | solution.py:356
  250.9 5.9 %copy-start.2 = (bf16[2,768,1280]{2,1,0:T(8,128)(2,1)S(1)}, bf16[2,768,1280]{2,1,0:T(8,128)(2,1)}, u32[]{:S(2)}) copy-start(bf16[2,768,1280]{2,1,0:T(8,128)(2,1)} %get-tuple-element.28) | copy-start | bytes 11796484
  252.7 4.1 collective-permute-start.4
  258.6 4.8 %collective-permute-start.8 = (bf16[96,384]{1,0:T(8,128)(2,1)}, bf16[96,384]{1,0:T(8,128)(2,1)S(1)}, u32[]{:S(2)}, u32[]{:S(2)}) collective-permute-start(bf16[96,384]{1,0:T(8,128)(2,1)} %reduce-scatter.7.cloned.1.call-done), channel_id=1, source_target_pairs={{0,16},{8,24},{16,0},{24,8},{1,17},{9,25},{17,1},{25,9},{2,18},{10... | collective-permute-start | bytes 221192 | tf_op jit(solution)/shard_map/ppermute | solution.py:358
  264.4 51.2 %collective-permute-start.9 = (bf16[96,384]{1,0:T(8,128)(2,1)S(1)}, bf16[96,384]{1,0:T(8,128)(2,1)S(1)}, u32[]{:S(2)}, u32[]{:S(2)}) collective-permute-start(bf16[96,384]{1,0:T(8,128)(2,1)S(1)} %add_convert_fusion.3), channel_id=1, source_target_pairs={{0,8},{8,0},{16,24},{24,16},{1,9},{9,1},{17,25},{25,17},{2,10},{10... | collective-permute-start | bytes 221192 | tf_op jit(solution)/shard_map/ppermute | solution.py:360
  314.1 5.0 %collective-permute-start.14 = (bf16[144,384]{1,0:T(8,128)(2,1)}, bf16[144,384]{1,0:T(8,128)(2,1)S(1)}, u32[]{:S(2)}, u32[]{:S(2)}) collective-permute-start(bf16[144,384]{1,0:T(8,128)(2,1)} %reduce-scatter.11.cloned.1.call-done), channel_id=1, source_target_pairs={{0,16},{8,24},{16,0},{24,8},{1,17},{9,25},{17,1},{25,9},{2,18},{10... | collective-permute-start | bytes 331784 | tf_op jit(solution)/shard_map/ppermute | solution.py:358
  320.0 65.0 %collective-permute-start.15 = (bf16[144,384]{1,0:T(8,128)(2,1)S(1)}, bf16[144,384]{1,0:T(8,128)(2,1)S(1)}, u32[]{:S(2)}, u32[]{:S(2)}) collective-permute-start(bf16[144,384]{1,0:T(8,128)(2,1)S(1)} %add_convert_fusion.2), channel_id=1, source_target_pairs={{0,8},{8,0},{16,24},{24,16},{1,9},{9,1},{17,25},{25,17},{2,10},{10... | collective-permute-start | bytes 331784 | tf_op jit(solution)/shard_map/ppermute | solution.py:360
  383.5 70.6 %collective-permute-start.11 = (bf16[96,1280]{1,0:T(8,128)(2,1)}, bf16[96,1280]{1,0:T(8,128)(2,1)S(1)}, u32[]{:S(2)}, u32[]{:S(2)}) collective-permute-start(bf16[96,1280]{1,0:T(8,128)(2,1)} %reduce-scatter.9.cloned.1.call-done), channel_id=1, source_target_pairs={{0,16},{8,24},{16,0},{24,8},{1,17},{9,25},{17,1},{25,9},{2,18},{10... | collective-permute-start | bytes 737288 | tf_op jit(solution)/shard_map/ppermute | solution.py:358
  452.5 6.4 %collective-permute-start.5 = (bf16[96,1280]{1,0:T(8,128)(2,1)}, bf16[96,1280]{1,0:T(8,128)(2,1)S(1)}, u32[]{:S(2)}, u32[]{:S(2)}) collective-permute-start(bf16[96,1280]{1,0:T(8,128)(2,1)} %reduce-scatter.5.cloned.1.call-done), channel_id=1, source_target_pairs={{0,16},{8,24},{16,0},{24,8},{1,17},{9,25},{17,1},{25,9},{2,18},{10... | collective-permute-start | bytes 737288 | tf_op jit(solution)/shard_map/ppermute | solution.py:358
  455.1 6.1 %collective-permute-start.12 = (bf16[96,1280]{1,0:T(8,128)(2,1)S(1)}, bf16[96,1280]{1,0:T(8,128)(2,1)S(1)}, u32[]{:S(2)}, u32[]{:S(2)}) collective-permute-start(bf16[96,1280]{1,0:T(8,128)(2,1)S(1)} %get-tuple-element.35), channel_id=1, source_target_pairs={{0,8},{8,0},{16,24},{24,16},{1,9},{9,1},{17,25},{25,17},{2,10},{10... | collective-permute-start | bytes 737288 | tf_op jit(solution)/shard_map/ppermute | solution.py:360
  459.9 2.4 collective-permute-start.6
  461.3 2.0 copy-start.1
Sparse Core Ops, SparseCore 0:
  10.8 56.2 all-gather.4
  69.8 45.8 all-gather.2
  188.1 61.3 reduce-scatter.6
  253.8 60.2 reduce-scatter.10
  317.8 65.6 reduce-scatter.8
  386.8 65.5 reduce-scatter.4

commit v2 on v1

--- a/solution.py
+++ b/solution.py
@@ -269,7 +269,7 @@
         in_specs=[WHOLE] * 5,
         out_specs=[WHOLE] * 4,
         compiler_params=PARAMS,
-        cost_estimate=cost(8_000_000_000, 14_000_000),
+        cost_estimate=cost(23_000_000_000, 14_000_000),
         name="attend",
     )(x, gain, w, cosine, sine)
 
@@ -296,7 +296,7 @@
             pltpu.VMEM((FF, D), F32), pltpu.VMEM((1, D), F32),
         ],
         compiler_params=PARAMS,
-        cost_estimate=cost(20_000_000_000, 25_000_000),
+        cost_estimate=cost(41_000_000_000, 25_000_000),
         name="ffn",
     )(x, att, cot, gain, wo, wi, wd)
 
@@ -310,7 +310,7 @@
         out_specs=WHOLE,
         scratch_shapes=[pltpu.VMEM((t, D), F32), pltpu.VMEM((t, D), F32)],
         compiler_params=PARAMS,
-        cost_estimate=cost(10_000_000_000, 14_000_000),
+        cost_estimate=cost(41_000_000_000, 14_000_000),
         name="back",
     )(q, k, v, gatt, cosine, sine)
 
@@ -325,12 +325,16 @@
         out_shape=[shape((t, D), BF16), shape((2, D, FF + 128), BF16)],
         scratch_shapes=[pltpu.VMEM((D, 3 * D), F32), pltpu.VMEM((1, D), F32)],
         compiler_params=PARAMS,
-        cost_estimate=cost(8_000_000_000, 20_000_000),
+        cost_estimate=cost(18_000_000_000, 20_000_000),
         name="last",
     )(x, after, gp, gain, w)
 
 
-def body(copies, tokens, gain_attn, w_qkv, w_out, gain_ffn, w_in, w_down, cotangent):
+def add(a, b):
+    return (a.astype(F32) + b.astype(F32)).astype(BF16)
+
+
+def body(copies, shards, tokens, gain_attn, w_qkv, w_out, gain_ffn, w_in, w_down, cotangent):
     core = lax.axis_index("replica") % 2
     to_core = [(r, r ^ 1) for r in range(copies)]
     to_chip = [(r, r ^ 2) for r in range(copies)]
@@ -344,44 +348,87 @@
         width = w.shape[1] // 2
         return lax.dynamic_slice_in_dim(w, core * width, width, 1)
 
-    def gather(w):
-        mine = lax.all_gather(w, "shard", axis=0, tiled=True)
-        return mine, lax.ppermute(mine, "replica", to_core)
-
-    def reduce_rows(g):
+    place = lax.axis_index("shard")
+    bits = shards.bit_length() - 1
+
+    def across(w, bit):
+        return lax.ppermute(w, "shard", [(i, i ^ (1 << bit)) for i in range(shards)])
+
+    def my_bit(bit):
+        return (place // (1 << bit)) % 2
+
+    def widen(w, bit):
+        other = across(w, bit)
+        low = my_bit(bit) == 0
+        return jnp.stack([jnp.where(low, w, other), jnp.where(low, other, w)], axis=-3)
+
+    def join(w, other):
+        low = my_bit(0) == 0
+        w = jnp.stack([jnp.where(low, w, other), jnp.where(low, other, w)], axis=-3)
+        w = w.reshape(-1, w.shape[-1])
+        return w, lax.ppermute(w, "replica", to_core)
+
+    def over_core(g):
+        rows, width = g.shape[1] // shards, g.shape[2]
         mine = lax.dynamic_index_in_dim(g, core, 0, keepdims=False)
         theirs = lax.dynamic_index_in_dim(g, 1 - core, 0, keepdims=False)
         theirs = lax.ppermute(theirs, "replica", to_core)
-        part = (mine.astype(F32) + theirs.astype(F32)).astype(BF16)
-        part = lax.psum_scatter(part, "shard", scatter_dimension=0, tiled=True)
-        for perm in () if copies < 4 else (to_chip,):
-            across = lax.ppermute(part, "replica", perm)
-            part = (part.astype(F32) + across.astype(F32)).astype(BF16)
+        return add(mine, theirs).reshape(shards, rows, width)
+
+    def over_bit(part, bit):
+        pairs = part.reshape((-1, 2) + part.shape[1:])
+        mine = lax.dynamic_index_in_dim(pairs, my_bit(bit), 1, keepdims=False)
+        theirs = lax.dynamic_index_in_dim(pairs, 1 - my_bit(bit), 1, keepdims=False)
+        return add(mine, across(theirs, bit))
+
+    def settle(part, done):
+        for bit in range(done, bits):
+            part = over_bit(part, bit)
+        part = part[0]
+        if copies == 4:
+            part = add(part, lax.ppermute(part, "replica", to_chip))
         other = lax.ppermute(part, "replica", to_core)
         return part.astype(F32), other.astype(F32)
 
     gains = jnp.stack([gain_attn, gain_ffn], axis=1)
     gains = jnp.pad(gains, ((0, 0), (0, 126)))
-    mine, other = gather(jnp.concatenate([half_of(w_qkv), gains], axis=1))
+    first = jnp.concatenate([half_of(w_qkv), gains], axis=1)
+    for bit in range(bits - 1, 0, -1):
+        first = widen(first, bit)
+    first, *rest = lax.optimization_barrier(
+        (first, half_of(w_in), half_of(w_down), half_of(w_out))
+    )
+    mine, other = join(first, across(first, 0))
+    for bit in range(bits - 1, 0, -1):
+        rest = [widen(w, bit) for w in rest]
     joint = in_order(mine[:, :FF], other[:, :FF])
     gain_one = mine[:, FF].astype(F32)[None, :]
     gain_two = mine[:, FF + 1].astype(F32)[None, :]
-    out_weight = in_order(*gather(half_of(w_out)))
-    in_weight = in_order(*gather(half_of(w_in)))
-    down_weight = in_order(*gather(half_of(w_down)))
 
     cosine, sine = rotary_tables(LENGTH)
+    joint, *rest = lax.optimization_barrier((joint, *rest))
+    arriving = [across(w, 0) for w in rest]
     q, k, v, att = attend(tokens, gain_one, joint, cosine, sine)
+    att, *arriving = lax.optimization_barrier((att, *arriving))
+    in_weight, down_weight, out_weight = (
+        in_order(*join(w, other)) for w, other in zip(rest, arriving)
+    )
     output, after, gatt, gout, gin, gdown = ffn(
         tokens, att, cotangent, gain_two, out_weight, in_weight, down_weight
     )
+    parts = [over_core(g) for g in (gin, gdown, gout)]
+    gatt, *parts = lax.optimization_barrier((gatt, *parts))
     gp = back(q, k, v, gatt, cosine, sine)
+    parts = [over_bit(part, 0) for part in parts]
+    gp, *parts = lax.optimization_barrier((gp, *parts))
     input_grad, gqkv = last(tokens, after, gp, gain_one, joint)
-
-    in_mine, in_other = reduce_rows(gin)
-    grad_down = in_order(*reduce_rows(gdown))
-    grad_out = in_order(*reduce_rows(gout))
-    qkv_mine, qkv_other = reduce_rows(gqkv)
+    parts = [over_bit(part, 1) for part in parts]
+    gqkv, *parts = lax.optimization_barrier((gqkv, *parts))
+
+    qkv_mine, qkv_other = settle(over_core(gqkv), 0)
+    in_mine, in_other = settle(parts[0], 2)
+    grad_down = in_order(*settle(parts[1], 2))
+    grad_out = in_order(*settle(parts[2], 2))
     return (
         output,
         input_grad,
@@ -396,7 +443,7 @@
 
 def solution(mesh):
     return jax.shard_map(
-        functools.partial(body, mesh.shape["replica"]),
+        functools.partial(body, mesh.shape["replica"], mesh.shape["shard"]),
         mesh=mesh,
         in_specs=(
             P(("replica", "shard"), None),

time: 471 us -> 317 us (0.67)
  waiting for transfers between devices: 227 us -> 122 us
  blocking collectives: 67.6 us -> 0 us
  starting transfers between devices: 8.92 us -> 40.7 us
  between operations: 14.4 us -> 1.32 us
    reduce_scatter x4 -> x0, waiting for transfers between devices: 179 us -> none  [reduce_rows(): part = lax.psum_scatter(part, 'shard', scatter_dimension=0, tiled=True)]
    ppermute x16 -> x40, waiting for transfers between devices: 16.7 us -> 122 us  [the longest x24 106 us: across(): return lax.ppermute(w, 'shard', [(i, i ^ 1 << bit) for i in range(shards)])]
    all_gather x2 -> x0, blocking collectives: 67.6 us -> none  [gather(): mine = lax.all_gather(w, 'shard', axis=0, tiled=True)]
    ppermute x16 -> x40, starting transfers between devices: 8.45 us -> 40.7 us  [the longest x24 35.5 us: across(): return lax.ppermute(w, 'shard', [(i, i ^ 1 << bit) for i in range(shards)])]
    all_gather x2 -> x0, waiting for transfers between devices: 30.8 us -> none  [gather(): mine = lax.all_gather(w, 'shard', axis=0, tiled=True)]
    convert_element_type x8 -> x16, other arithmetic: 12.1 us -> 9.39 us  [the longest x14 9.27 us: add(): return (a.astype(F32) + b.astype(F32)).astype(BF16)]
  transfers between devices with their start and end apart: 22 -> 40, of which waited for: 9 -> 19; matrix products, arithmetic and copies ran while one was open for 8% -> 8% of each run, Pallas kernels for 11% -> 23%
where the time goes in v2:
time: 317 us
  waiting for transfers between devices  122 us (38%)
  Pallas kernels  108 us (34%)
  starting transfers between devices  40.7 us (13%)
  other arithmetic  31.2 us (10%)
  local copies, waits for them, and re-layouts  12.9 us (4%)
    ppermute x24, waiting for transfers between devices, across(): return lax.ppermute(w, 'shard', [(i, i ^ 1 << bit) for i in range(shards)])  106 us
    pallas_call x1, Pallas kernels, back(): pl.pallas_call(back_kernel, out_shape=shape((t, 3 * D), BF16), in_specs=[...  35.9 us
    pallas_call x1, Pallas kernels, ffn(): pl.pallas_call(ffn_kernel, grid=(t // ROWS,), in_specs=[by_rows(D), by_ro...  35.8 us
    ppermute x24, starting transfers between devices, across(): return lax.ppermute(w, 'shard', [(i, i ^ 1 << bit) for i in range(shards)])  35.5 us
    pallas_call x1, Pallas kernels, attend(): pl.pallas_call(attend_kernel, out_shape=[shape((t, D), BF16)] * 4, in_spe...  20.5 us
    pallas_call x1, Pallas kernels, last(): pl.pallas_call(last_kernel, grid=(t // ROWS,), in_specs=[by_rows(D), by_r...  16.2 us
    ppermute x4, waiting for transfers between devices, settle(): part = add(part, lax.ppermute(part, 'replica', to_chip))  10.4 us
    concatenate x8, other arithmetic, in_order(): jnp.concatenate([jnp.where(core == 0, mine, other), jnp.where(core == 0,...  10.1 us
  transfers between devices with their start and end apart: 40, of which 19 were waited for; matrix products, arithmetic and copies ran while one was open for 8% of the time, Pallas kernels for 23%

profile of v2, /device:TPU:0, one launch (start us, length us, event | category | flops | bytes accessed | tf_op | source)
XLA Modules:
  0.0 316.7 jit_solution(3496033128958490410)
XLA Ops:
  1.7 4.1 %collective-permute-start = (bf16[96,1280]{1,0:T(8,128)(2,1)S(1)}, bf16[96,1280]{1,0:T(8,128)(2,1)S(1)}, u32[]{:S(2)}, u32[]{:S(2)}) collective-permute-start(bf16[96,1280]{1,0:T(8,128)(2,1)S(1)} %fusion.13), channel_id=1, source_target_pairs={{0,4},{1,5},{2,6},{3,7},{4,0},{5,1},{6,2},{7,3},{8,12},{9,13},{10,... | collective-permute-start | bytes 737288 | tf_op jit(solution)/shard_map/ppermute | solution.py:355
  5.8 11.2 %collective-permute-done = bf16[96,1280]{1,0:T(8,128)(2,1)S(1)} collective-permute-done((bf16[96,1280]{1,0:T(8,128)(2,1)S(1)}, bf16[96,1280]{1,0:T(8,128)(2,1)S(1)}, u32[]{:S(2)}, u32[]{:S(2)}) %collective-permute-start) | collective-permute-done | bytes 245792 | tf_op jit(solution)/shard_map/ppermute | solution.py:355
  18.1 11.6 %collective-permute-done.1 = bf16[2,96,1280]{2,1,0:T(8,128)(2,1)S(1)} collective-permute-done((bf16[2,96,1280]{2,1,0:T(8,128)(2,1)S(1)}, bf16[2,96,1280]{2,1,0:T(8,128)(2,1)S(1)}, u32[]{:S(2)}, u32[]{:S(2)}) %collective-permute-start.1) | collective-permute-done | bytes 491552 | tf_op jit(solution)/shard_map/ppermute | solution.py:355
  31.2 1.9 fusion.16
  33.1 3.4 %collective-permute-start.8 = (bf16[96,384]{1,0:T(8,128)(2,1)S(1)}, bf16[96,384]{1,0:T(8,128)(2,1)S(1)}, u32[]{:S(2)}, u32[]{:S(2)}) collective-permute-start(bf16[96,384]{1,0:T(8,128)(2,1)S(1)} %constant_dynamic-slice_fusion.4), channel_id=1, source_target_pairs={{0,4},{1,5},{2,6},{3,7},{4,0},{5,1},{6,2},{7,3},{8,12},{9,13},{10,... | collective-permute-start | bytes 221192 | tf_op jit(solution)/shard_map/ppermute | solution.py:355
  36.5 1.8 pad_maximum_fusion.12
  38.3 2.9 collective-permute-start.4
  41.3 6.7 %collective-permute-start.9 = (bf16[2,96,384]{2,1,0:T(8,128)(2,1)S(1)}, bf16[2,96,384]{2,1,0:T(8,128)(2,1)S(1)}, u32[]{:S(2)}, u32[]{:S(2)}) collective-permute-start(bf16[2,96,384]{2,1,0:T(8,128)(2,1)S(1)} %pad_maximum_fusion.21), channel_id=1, source_target_pairs={{0,2},{1,3},{2,0},{3,1},{4,6},{5,7},{6,4},{7,5},{8,10},{9,11},{10,... | collective-permute-start | bytes 442376 | tf_op jit(solution)/shard_map/ppermute | solution.py:355
  48.1 3.3 %collective-permute-done.6 = bf16[144,384]{1,0:T(8,128)(2,1)S(1)} collective-permute-done((bf16[144,384]{1,0:T(8,128)(2,1)S(1)}, bf16[144,384]{1,0:T(8,128)(2,1)S(1)}, u32[]{:S(2)}, u32[]{:S(2)}) %collective-permute-start.6) | collective-permute-done | bytes 110624 | tf_op jit(solution)/shard_map/ppermute | solution.py:355
  52.5 2.6 collective-permute-done.4
  56.9 4.7 %collective-permute-done.7 = bf16[2,144,384]{2,1,0:T(8,128)(2,1)S(1)} collective-permute-done((bf16[2,144,384]{2,1,0:T(8,128)(2,1)S(1)}, bf16[2,144,384]{2,1,0:T(8,128)(2,1)S(1)}, u32[]{:S(2)}, u32[]{:S(2)}) %collective-permute-start.7) | collective-permute-done | bytes 221216 | tf_op jit(solution)/shard_map/ppermute | solution.py:355
  61.7 8.4 %collective-permute-done.5 = bf16[2,96,1152]{2,1,0:T(8,128)(2,1)S(1)} collective-permute-done((bf16[2,96,1152]{2,1,0:T(8,128)(2,1)S(1)}, bf16[2,96,1152]{2,1,0:T(8,128)(2,1)S(1)}, u32[]{:S(2)}, u32[]{:S(2)}) %collective-permute-start.5) | collective-permute-done | bytes 442400 | tf_op jit(solution)/shard_map/ppermute | solution.py:355
  71.4 2.1 pad_maximum_fusion.w_ref
  76.1 20.5 %attend.1 = (bf16[1024,768]{1,0:T(8,128)(2,1)}, bf16[1024,768]{1,0:T(8,128)(2,1)}, bf16[1024,768]{1,0:T(8,128)(2,1)}, bf16[1024,768]{1,0:T(8,128)(2,1)}) custom-call(bf16[1024,768]{1,0:T(8,128)(2,1)} %x_ref.5, f32[1,768]{1,0:T(1,128)} %reshape.159.gain_ref, bf16[768,2304]{1,0:T(8,128)(2,1)} %pad_maximum_fusion.w_ref, ...), custom_call_target="tpu_custom_call" | custom-call | flops 23000000512 | bytes 14000000 | tf_op jit(solution)/shard_map/attend/pallas_call | solution.py:266
  96.5 13.5 %collective-permute-done.12 = bf16[2,2,96,384]{3,2,0,1:T(8,128)(2,1)S(1)} collective-permute-done((bf16[2,2,96,384]{3,2,0,1:T(8,128)(2,1)S(1)}, bf16[2,2,96,384]{3,2,0,1:T(8,128)(2,1)S(1)}, u32[]{:S(2)}, u32[]{:S(2)}) %collective-permute-start.12) | collective-permute-done | bytes 294944 | tf_op jit(solution)/shard_map/ppermute | solution.py:355
  121.3 2.0 pad_maximum_fusion.1.wi_ref
  123.3 35.8 %ffn.1 = (bf16[1024,768]{1,0:T(8,128)(2,1)}, f32[1024,768]{1,0:T(8,128)}, bf16[1024,768]{1,0:T(8,128)(2,1)}, bf16[2,768,384]{2,1,0:T(8,128)(2,1)}, bf16[2,768,12...) custom-call(bf16[1024,768]{1,0:T(8,128)(2,1)} %x_ref.5, bf16[1024,768]{1,0:T(8,128)(2,1)} %get-tuple-element.53.att_ref, ...), custom_call_target="tpu_custom_call" | custom-call | flops 41000001536 | bytes 25000000 | tf_op jit(solution)/shard_map/ffn/pallas_call | solution.py:279
  159.1 3.2 %dynamic-slice_bitcast_fusion.1 = bf16[768,1280]{1,0:T(8,128)(2,1)} fusion(bf16[2,768,1280]{2,1,0:T(8,128)(2,1)} %get-tuple-element.63, s32[]{:T(128)S(6)} %select_n.482), kind=kLoop, calls=%fused_computation.12 | loop fusion | bytes 3932164 | tf_op jit(solution)/shard_map/jit(dynamic_index_in_dim)/squeeze | solution.py:374
  163.2 4.7 %collective-permute-done.18 = bf16[768,384]{1,0:T(8,128)(2,1)S(1)} collective-permute-done((bf16[768,384]{1,0:T(8,128)(2,1)S(1)}, bf16[768,384]{1,0:T(8,128)(2,1)S(1)}, u32[]{:S(2)}, u32[]{:S(2)}) %collective-permute-start.18) | collective-permute-done | bytes 589856 | tf_op jit(solution)/shard_map/ppermute | solution.py:375
  170.2 2.1 fusion.1
  176.7 35.9 %back.1.gp_ref = bf16[1024,2304]{1,0:T(8,128)(2,1)} custom-call(bf16[1024,768]{1,0:T(8,128)(2,1)} %get-tuple-element.59.q_ref, bf16[1024,768]{1,0:T(8,128)(2,1)} %get-tuple-element.60.k_ref, bf16[1024,768]{1,0:T(8,128)(2,1)} %get-tuple-element.61.v_ref, bf16[1024,768]{1,0:T(8,128)(2,1)} %get-tuple-element.66.gatt_ref, ...), custom_call_target="tpu_custom_call" | custom-call | flops 41000001536 | bytes 14000000 | tf_op jit(solution)/shard_map/back/pallas_call | solution.py:306
  215.4 2.1 collective-permute-start.23
  217.6 16.2 %last.1 = (bf16[1024,768]{1,0:T(8,128)(2,1)}, bf16[2,768,1280]{2,1,0:T(8,128)(2,1)}) custom-call(bf16[1024,768]{1,0:T(8,128)(2,1)} %x_ref.5, f32[1024,768]{1,0:T(8,128)} %get-tuple-element.58.after_ref, bf16[1024,2304]{1,0:T(8,128)(2,1)} %back.1.gp_ref, f32[1,768]{1,0:T(1,128)} %reshape.159.gain_ref, bf16[768,2304]{1,0:T(8,128)(2,1)} %pad_maximum_fusion.w_ref), custom_call_target="tpu_custom_call" | custom-call | flops 17999998976 | bytes 20000000 | tf_op jit(solution)/shard_map/last/pallas_call | solution.py:320
  235.8 3.0 dynamic-slice_bitcast_fusion
  243.6 12.7 %collective-permute-done.31 = bf16[1,96,384]{2,1,0:T(8,128)(2,1)S(1)} collective-permute-done((bf16[1,96,384]{2,1,0:T(8,128)(2,1)S(1)}, bf16[1,96,384]{2,1,0:T(8,128)(2,1)S(1)}, u32[]{:S(2)}, u32[]{:S(2)}) %collective-permute-start.31) | collective-permute-done | bytes 73760 | tf_op jit(solution)/shard_map/ppermute | solution.py:355
  257.9 2.0 fusion
  262.4 4.1 %collective-permute-done.38 = bf16[144,384]{1,0:T(8,128)(2,1)S(1)} collective-permute-done((bf16[144,384]{1,0:T(8,128)(2,1)S(1)}, bf16[144,384]{1,0:T(8,128)(2,1)S(1)}, u32[]{:S(2)}, u32[]{:S(2)}) %collective-permute-start.38) | collective-permute-done | bytes 110624 | tf_op jit(solution)/shard_map/ppermute | solution.py:389
  267.4 15.6 %collective-permute-done.26 = bf16[4,96,1280]{2,1,0:T(8,128)(2,1)S(1)} collective-permute-done((bf16[4,96,1280]{2,1,0:T(8,128)(2,1)S(1)}, bf16[4,96,1280]{2,1,0:T(8,128)(2,1)S(1)}, u32[]{:S(2)}, u32[]{:S(2)}) %collective-permute-start.26) | collective-permute-done | bytes 983072 | tf_op jit(solution)/shard_map/ppermute | solution.py:355
  284.9 9.9 %collective-permute-done.27 = bf16[2,96,1280]{2,1,0:T(8,128)(2,1)S(1)} collective-permute-done((bf16[2,96,1280]{2,1,0:T(8,128)(2,1)S(1)}, bf16[2,96,1280]{2,1,0:T(8,128)(2,1)S(1)}, u32[]{:S(2)}, u32[]{:S(2)}) %collective-permute-start.27) | collective-permute-done | bytes 491552 | tf_op jit(solution)/shard_map/ppermute | solution.py:355
  295.0 2.3 collective-permute-start.28
  298.0 8.9 %collective-permute-done.28 = bf16[1,96,1280]{2,1,0:T(8,128)(2,1)S(1)} collective-permute-done((bf16[1,96,1280]{2,1,0:T(8,128)(2,1)S(1)}, bf16[1,96,1280]{2,1,0:T(8,128)(2,1)S(1)}, u32[]{:S(2)}, u32[]{:S(2)}) %collective-permute-start.28) | collective-permute-done | bytes 245792 | tf_op jit(solution)/shard_map/ppermute | solution.py:355
  307.6 6.3 %collective-permute-done.29 = bf16[96,1280]{1,0:T(8,128)(2,1)S(1)} collective-permute-done((bf16[96,1280]{1,0:T(8,128)(2,1)S(1)}, bf16[96,1280]{1,0:T(8,128)(2,1)S(1)}, u32[]{:S(2)}, u32[]{:S(2)}) %collective-permute-start.29) | collective-permute-done | bytes 245792 | tf_op jit(solution)/shard_map/ppermute | solution.py:389
  (168 shorter events, 50.1 us)
Async XLA Ops:
  1.7 15.3 %collective-permute-start = (bf16[96,1280]{1,0:T(8,128)(2,1)S(1)}, bf16[96,1280]{1,0:T(8,128)(2,1)S(1)}, u32[]{:S(2)}, u32[]{:S(2)}) collective-permute-start(bf16[96,1280]{1,0:T(8,128)(2,1)S(1)} %fusion.13), channel_id=1, source_target_pairs={{0,4},{1,5},{2,6},{3,7},{4,0},{5,1},{6,2},{7,3},{8,12},{9,13},{10,... | collective-permute-start | bytes 737288 | tf_op jit(solution)/shard_map/ppermute | solution.py:355
  17.2 12.5 %collective-permute-start.1 = (bf16[2,96,1280]{2,1,0:T(8,128)(2,1)S(1)}, bf16[2,96,1280]{2,1,0:T(8,128)(2,1)S(1)}, u32[]{:S(2)}, u32[]{:S(2)}) collective-permute-start(bf16[2,96,1280]{2,1,0:T(8,128)(2,1)S(1)} %pad_maximum_fusion.14), channel_id=1, source_target_pairs={{0,2},{1,3},{2,0},{3,1},{4,6},{5,7},{6,4},{7,5},{8,10},{9,11},{10,... | collective-permute-start | bytes 1474568 | tf_op jit(solution)/shard_map/ppermute | solution.py:355
  29.8 22.1 %collective-permute-start.2 = (bf16[2,2,96,1280]{3,2,0,1:T(8,128)(2,1)S(1)}, bf16[2,2,96,1280]{3,2,0,1:T(8,128)(2,1)S(1)}, u32[]{:S(2)}, u32[]{:S(2)}) collective-permute-start(bf16[2,2,96,1280]{3,2,0,1:T(8,128)(2,1)S(1)} %pad_maximum_fusion.6), channel_id=1, source_target_pairs={{0,1},{1,0},{2,3},{3,2},{4,5},{5,4},{6,7},{7,6},{8,9},{9,8},{10,11... | collective-permute-start | bytes 2949128 | tf_op jit(solution)/shard_map/ppermute | solution.py:355
  33.1 8.2 %collective-permute-start.8 = (bf16[96,384]{1,0:T(8,128)(2,1)S(1)}, bf16[96,384]{1,0:T(8,128)(2,1)S(1)}, u32[]{:S(2)}, u32[]{:S(2)}) collective-permute-start(bf16[96,384]{1,0:T(8,128)(2,1)S(1)} %constant_dynamic-slice_fusion.4), channel_id=1, source_target_pairs={{0,4},{1,5},{2,6},{3,7},{4,0},{5,1},{6,2},{7,3},{8,12},{9,13},{10,... | collective-permute-start | bytes 221192 | tf_op jit(solution)/shard_map/ppermute | solution.py:355
  38.3 13.0 %collective-permute-start.6 = (bf16[144,384]{1,0:T(8,128)(2,1)S(1)}, bf16[144,384]{1,0:T(8,128)(2,1)S(1)}, u32[]{:S(2)}, u32[]{:S(2)}) collective-permute-start(bf16[144,384]{1,0:T(8,128)(2,1)S(1)} %constant_dynamic-slice_fusion.5), channel_id=1, source_target_pairs={{0,4},{1,5},{2,6},{3,7},{4,0},{5,1},{6,2},{7,3},{8,12},{9,13},{10,... | collective-permute-start | bytes 331784 | tf_op jit(solution)/shard_map/ppermute | solution.py:355
  38.3 16.7 %collective-permute-start.4 = (bf16[96,1152]{1,0:T(8,128)(2,1)S(1)}, bf16[96,1152]{1,0:T(8,128)(2,1)S(1)}, u32[]{:S(2)}, u32[]{:S(2)}) collective-permute-start(bf16[96,1152]{1,0:T(8,128)(2,1)S(1)} %constant_dynamic-slice_fusion.6), channel_id=1, source_target_pairs={{0,4},{1,5},{2,6},{3,7},{4,0},{5,1},{6,2},{7,3},{8,12},{9,13},{10,... | collective-permute-start | bytes 663560 | tf_op jit(solution)/shard_map/ppermute | solution.py:355
  41.3 15.5 %collective-permute-start.9 = (bf16[2,96,384]{2,1,0:T(8,128)(2,1)S(1)}, bf16[2,96,384]{2,1,0:T(8,128)(2,1)S(1)}, u32[]{:S(2)}, u32[]{:S(2)}) collective-permute-start(bf16[2,96,384]{2,1,0:T(8,128)(2,1)S(1)} %pad_maximum_fusion.21), channel_id=1, source_target_pairs={{0,2},{1,3},{2,0},{3,1},{4,6},{5,7},{6,4},{7,5},{8,10},{9,11},{10,... | collective-permute-start | bytes 442376 | tf_op jit(solution)/shard_map/ppermute | solution.py:355
  51.4 10.1 %collective-permute-start.7 = (bf16[2,144,384]{2,1,0:T(8,128)(2,1)S(1)}, bf16[2,144,384]{2,1,0:T(8,128)(2,1)S(1)}, u32[]{:S(2)}, u32[]{:S(2)}) collective-permute-start(bf16[2,144,384]{2,1,0:T(8,128)(2,1)S(1)} %pad_maximum_fusion.20), channel_id=1, source_target_pairs={{0,2},{1,3},{2,0},{3,1},{4,6},{5,7},{6,4},{7,5},{8,10},{9,11},{10,... | collective-permute-start | bytes 663560 | tf_op jit(solution)/shard_map/ppermute | solution.py:355
  52.4 18.7 %collective-permute-start.3 = (bf16[768,1280]{1,0:T(8,128)(2,1)S(1)}, bf16[768,1280]{1,0:T(8,128)(2,1)S(1)}, u32[]{:S(2)}, u32[]{:S(2)}) collective-permute-start(bf16[768,1280]{1,0:T(8,128)(2,1)S(1)} %bitcast.143), channel_id=1, source_target_pairs={{0,8},{8,0},{16,24},{24,16},{1,9},{9,1},{17,25},{25,17},{2,10},{10... | collective-permute-start | bytes 5898248 | tf_op jit(solution)/shard_map/ppermute | solution.py:369
  55.2 14.8 %collective-permute-start.5 = (bf16[2,96,1152]{2,1,0:T(8,128)(2,1)S(1)}, bf16[2,96,1152]{2,1,0:T(8,128)(2,1)S(1)}, u32[]{:S(2)}, u32[]{:S(2)}) collective-permute-start(bf16[2,96,1152]{2,1,0:T(8,128)(2,1)S(1)} %pad_maximum_fusion.15), channel_id=1, source_target_pairs={{0,2},{1,3},{2,0},{3,1},{4,6},{5,7},{6,4},{7,5},{8,10},{9,11},{10,... | collective-permute-start | bytes 1327112 | tf_op jit(solution)/shard_map/ppermute | solution.py:355
  73.5 36.5 %collective-permute-start.10 = (bf16[2,2,96,1152]{3,2,0,1:T(8,128)(2,1)S(1)}, bf16[2,2,96,1152]{3,2,0,1:T(8,128)(2,1)S(1)}, u32[]{:S(2)}, u32[]{:S(2)}) collective-permute-start(bf16[2,2,96,1152]{3,2,0,1:T(8,128)(2,1)S(1)} %pad_maximum_fusion.7), channel_id=1, source_target_pairs={{0,1},{1,0},{2,3},{3,2},{4,5},{5,4},{6,7},{7,6},{8,9},{9,8},{10,11... | collective-permute-start | bytes 2654216 | tf_op jit(solution)/shard_map/ppermute | solution.py:355
  74.0 36.0 %collective-permute-start.11 = (bf16[2,2,144,384]{3,2,0,1:T(8,128)(2,1)S(1)}, bf16[2,2,144,384]{3,2,0,1:T(8,128)(2,1)S(1)}, u32[]{:S(2)}, u32[]{:S(2)}) collective-permute-start(bf16[2,2,144,384]{3,2,0,1:T(8,128)(2,1)S(1)} %pad_maximum_fusion.16), channel_id=1, source_target_pairs={{0,1},{1,0},{2,3},{3,2},{4,5},{5,4},{6,7},{7,6},{8,9},{9,8},{10,11... | collective-permute-start | bytes 1327112 | tf_op jit(solution)/shard_map/ppermute | solution.py:355
  75.5 34.4 %collective-permute-start.12 = (bf16[2,2,96,384]{3,2,0,1:T(8,128)(2,1)S(1)}, bf16[2,2,96,384]{3,2,0,1:T(8,128)(2,1)S(1)}, u32[]{:S(2)}, u32[]{:S(2)}) collective-permute-start(bf16[2,2,96,384]{3,2,0,1:T(8,128)(2,1)S(1)} %pad_maximum_fusion.18), channel_id=1, source_target_pairs={{0,1},{1,0},{2,3},{3,2},{4,5},{5,4},{6,7},{7,6},{8,9},{9,8},{10,11... | collective-permute-start | bytes 884744 | tf_op jit(solution)/shard_map/ppermute | solution.py:355
  112.5 7.0 %collective-permute-start.14 = (bf16[768,1152]{1,0:T(8,128)(2,1)S(1)}, bf16[768,1152]{1,0:T(8,128)(2,1)}, u32[]{:S(2)}, u32[]{:S(2)}) collective-permute-start(bf16[768,1152]{1,0:T(8,128)(2,1)S(1)} %bitcast.150), channel_id=1, source_target_pairs={{0,8},{8,0},{16,24},{24,16},{1,9},{9,1},{17,25},{25,17},{2,10},{10... | collective-permute-start | bytes 5308424 | tf_op jit(solution)/shard_map/ppermute | solution.py:369
  162.3 7.9 %collective-permute-start.16 = (bf16[768,1280]{1,0:T(8,128)(2,1)}, bf16[768,1280]{1,0:T(8,128)(2,1)}, u32[]{:S(2)}, u32[]{:S(2)}) collective-permute-start(bf16[768,1280]{1,0:T(8,128)(2,1)} %dynamic-slice_bitcast_fusion.1), channel_id=1, source_target_pairs={{0,8},{8,0},{16,24},{24,16},{1,9},{9,1},{17,25},{25,17},{2,10},{10... | collective-permute-start | bytes 5898248 | tf_op jit(solution)/shard_map/ppermute | solution.py:375
  172.3 40.3 %collective-permute-start.21 = (bf16[4,96,384]{2,1,0:T(8,128)(2,1)S(1)}, bf16[4,96,384]{2,1,0:T(8,128)(2,1)S(1)}, u32[]{:S(2)}, u32[]{:S(2)}) collective-permute-start(bf16[4,96,384]{2,1,0:T(8,128)(2,1)S(1)} %dynamic-slice_bitcast_fusion.9), channel_id=1, source_target_pairs={{0,1},{1,0},{2,3},{3,2},{4,5},{5,4},{6,7},{7,6},{8,9},{9,8},{10,11... | collective-permute-start | bytes 884744 | tf_op jit(solution)/shard_map/ppermute | solution.py:355
  173.7 39.0 %collective-permute-start.20 = (bf16[4,144,384]{2,1,0:T(8,128)(2,1)}, bf16[4,144,384]{2,1,0:T(8,128)(2,1)}, u32[]{:S(2)}, u32[]{:S(2)}) collective-permute-start(bf16[4,144,384]{2,1,0:T(8,128)(2,1)} %dynamic-slice_bitcast_fusion.8), channel_id=1, source_target_pairs={{0,1},{1,0},{2,3},{3,2},{4,5},{5,4},{6,7},{7,6},{8,9},{9,8},{10,11... | collective-permute-start | bytes 1327112 | tf_op jit(solution)/shard_map/ppermute | solution.py:355
  176.2 37.6 %collective-permute-start.19 = (bf16[4,96,1280]{2,1,0:T(8,128)(2,1)}, bf16[4,96,1280]{2,1,0:T(8,128)(2,1)}, u32[]{:S(2)}, u32[]{:S(2)}) collective-permute-start(bf16[4,96,1280]{2,1,0:T(8,128)(2,1)} %dynamic-slice_bitcast_fusion.3), channel_id=1, source_target_pairs={{0,1},{1,0},{2,3},{3,2},{4,5},{5,4},{6,7},{7,6},{8,9},{9,8},{10,11... | collective-permute-start | bytes 2949128 | tf_op jit(solution)/shard_map/ppermute | solution.py:355
  215.3 18.5 %collective-permute-start.24 = (bf16[2,96,384]{2,1,0:T(8,128)(2,1)S(1)}, bf16[2,96,384]{2,1,0:T(8,128)(2,1)S(1)}, u32[]{:S(2)}, u32[]{:S(2)}) collective-permute-start(bf16[2,96,384]{2,1,0:T(8,128)(2,1)S(1)} %dynamic-slice_bitcast_fusion.11), channel_id=1, source_target_pairs={{0,2},{1,3},{2,0},{3,1},{4,6},{5,7},{6,4},{7,5},{8,10},{9,11},{10,... | collective-permute-start | bytes 442376 | tf_op jit(solution)/shard_map/ppermute | solution.py:355
  215.4 18.4 %collective-permute-start.23 = (bf16[2,144,384]{2,1,0:T(8,128)(2,1)S(1)}, bf16[2,144,384]{2,1,0:T(8,128)(2,1)S(1)}, u32[]{:S(2)}, u32[]{:S(2)}) collective-permute-start(bf16[2,144,384]{2,1,0:T(8,128)(2,1)S(1)} %dynamic-slice_bitcast_fusion.10), channel_id=1, source_target_pairs={{0,2},{1,3},{2,0},{3,1},{4,6},{5,7},{6,4},{7,5},{8,10},{9,11},{10,... | collective-permute-start | bytes 663560 | tf_op jit(solution)/shard_map/ppermute | solution.py:355
  217.5 18.2 %collective-permute-start.22 = (bf16[2,96,1280]{2,1,0:T(8,128)(2,1)S(1)}, bf16[2,96,1280]{2,1,0:T(8,128)(2,1)S(1)}, u32[]{:S(2)}, u32[]{:S(2)}) collective-permute-start(bf16[2,96,1280]{2,1,0:T(8,128)(2,1)S(1)} %dynamic-slice_bitcast_fusion.7), channel_id=1, source_target_pairs={{0,2},{1,3},{2,0},{3,1},{4,6},{5,7},{6,4},{7,5},{8,10},{9,11},{10,... | collective-permute-start | bytes 1474568 | tf_op jit(solution)/shard_map/ppermute | solution.py:355
  238.8 19.1 %collective-permute-start.25 = (bf16[768,1280]{1,0:T(8,128)(2,1)}, bf16[768,1280]{1,0:T(8,128)(2,1)S(1)}, u32[]{:S(2)}, u32[]{:S(2)}) collective-permute-start(bf16[768,1280]{1,0:T(8,128)(2,1)} %dynamic-slice_bitcast_fusion), channel_id=1, source_target_pairs={{0,8},{8,0},{16,24},{24,16},{1,9},{9,1},{17,25},{25,17},{2,10},{10... | collective-permute-start | bytes 5898248 | tf_op jit(solution)/shard_map/ppermute | solution.py:375
  238.8 22.8 %collective-permute-start.37 = (bf16[1,144,384]{2,1,0:T(8,128)(2,1)S(1)}, bf16[1,144,384]{2,1,0:T(8,128)(2,1)S(1)}, u32[]{:S(2)}, u32[]{:S(2)}) collective-permute-start(bf16[1,144,384]{2,1,0:T(8,128)(2,1)S(1)} %constant_dynamic-slice_fusion), channel_id=1, source_target_pairs={{0,4},{1,5},{2,6},{3,7},{4,0},{5,1},{6,2},{7,3},{8,12},{9,13},{10,... | collective-permute-start | bytes 331784 | tf_op jit(solution)/shard_map/ppermute | solution.py:355
  240.5 15.8 %collective-permute-start.31 = (bf16[1,96,384]{2,1,0:T(8,128)(2,1)S(1)}, bf16[1,96,384]{2,1,0:T(8,128)(2,1)S(1)}, u32[]{:S(2)}, u32[]{:S(2)}) collective-permute-start(bf16[1,96,384]{2,1,0:T(8,128)(2,1)S(1)} %constant_dynamic-slice_fusion.2), channel_id=1, source_target_pairs={{0,4},{1,5},{2,6},{3,7},{4,0},{5,1},{6,2},{7,3},{8,12},{9,13},{10,... | collective-permute-start | bytes 221192 | tf_op jit(solution)/shard_map/ppermute | solution.py:355
  241.9 41.5 %collective-permute-start.34 = (bf16[1,96,1280]{2,1,0:T(8,128)(2,1)S(1)}, bf16[1,96,1280]{2,1,0:T(8,128)(2,1)S(1)}, u32[]{:S(2)}, u32[]{:S(2)}) collective-permute-start(bf16[1,96,1280]{2,1,0:T(8,128)(2,1)S(1)} %constant_dynamic-slice_fusion.1), channel_id=1, source_target_pairs={{0,4},{1,5},{2,6},{3,7},{4,0},{5,1},{6,2},{7,3},{8,12},{9,13},{10,... | collective-permute-start | bytes 737288 | tf_op jit(solution)/shard_map/ppermute | solution.py:355
  260.0 23.0 %collective-permute-start.26 = (bf16[4,96,1280]{2,1,0:T(8,128)(2,1)S(1)}, bf16[4,96,1280]{2,1,0:T(8,128)(2,1)S(1)}, u32[]{:S(2)}, u32[]{:S(2)}) collective-permute-start(bf16[4,96,1280]{2,1,0:T(8,128)(2,1)S(1)} %dynamic-slice_bitcast_fusion.2), channel_id=1, source_target_pairs={{0,1},{1,0},{2,3},{3,2},{4,5},{5,4},{6,7},{7,6},{8,9},{9,8},{10,11... | collective-permute-start | bytes 2949128 | tf_op jit(solution)/shard_map/ppermute | solution.py:355
  266.5 17.6 %collective-permute-start.39 = (bf16[144,384]{1,0:T(8,128)(2,1)S(1)}, bf16[144,384]{1,0:T(8,128)(2,1)S(1)}, u32[]{:S(2)}, u32[]{:S(2)}) collective-permute-start(bf16[144,384]{1,0:T(8,128)(2,1)S(1)} %add_convert_fusion.4), channel_id=1, source_target_pairs={{0,8},{8,0},{16,24},{24,16},{1,9},{9,1},{17,25},{25,17},{2,10},{10... | collective-permute-start | bytes 331784 | tf_op jit(solution)/shard_map/ppermute | solution.py:390
  283.3 11.5 %collective-permute-start.27 = (bf16[2,96,1280]{2,1,0:T(8,128)(2,1)S(1)}, bf16[2,96,1280]{2,1,0:T(8,128)(2,1)S(1)}, u32[]{:S(2)}, u32[]{:S(2)}) collective-permute-start(bf16[2,96,1280]{2,1,0:T(8,128)(2,1)S(1)} %dynamic-slice_bitcast_fusion.6), channel_id=1, source_target_pairs={{0,2},{1,3},{2,0},{3,1},{4,6},{5,7},{6,4},{7,5},{8,10},{9,11},{10,... | collective-permute-start | bytes 1474568 | tf_op jit(solution)/shard_map/ppermute | solution.py:355
  283.5 13.8 %collective-permute-start.35 = (bf16[96,1280]{1,0:T(8,128)(2,1)S(1)}, bf16[96,1280]{1,0:T(8,128)(2,1)S(1)}, u32[]{:S(2)}, u32[]{:S(2)}) collective-permute-start(bf16[96,1280]{1,0:T(8,128)(2,1)S(1)} %fusion.15), channel_id=1, source_target_pairs={{0,16},{8,24},{16,0},{24,8},{1,17},{9,25},{17,1},{25,9},{2,18},{10... | collective-permute-start | bytes 737288 | tf_op jit(solution)/shard_map/ppermute | solution.py:389
  295.0 11.9 %collective-permute-start.28 = (bf16[1,96,1280]{2,1,0:T(8,128)(2,1)S(1)}, bf16[1,96,1280]{2,1,0:T(8,128)(2,1)S(1)}, u32[]{:S(2)}, u32[]{:S(2)}) collective-permute-start(bf16[1,96,1280]{2,1,0:T(8,128)(2,1)S(1)} %constant_dynamic-slice_fusion.3), channel_id=1, source_target_pairs={{0,4},{1,5},{2,6},{3,7},{4,0},{5,1},{6,2},{7,3},{8,12},{9,13},{10,... | collective-permute-start | bytes 737288 | tf_op jit(solution)/shard_map/ppermute | solution.py:355
  297.3 10.2 %collective-permute-start.36 = (bf16[96,1280]{1,0:T(8,128)(2,1)S(1)}, bf16[96,1280]{1,0:T(8,128)(2,1)S(1)}, u32[]{:S(2)}, u32[]{:S(2)}) collective-permute-start(bf16[96,1280]{1,0:T(8,128)(2,1)S(1)} %get-tuple-element.83), channel_id=1, source_target_pairs={{0,8},{8,0},{16,24},{24,16},{1,9},{9,1},{17,25},{25,17},{2,10},{10... | collective-permute-start | bytes 737288 | tf_op jit(solution)/shard_map/ppermute | solution.py:390
  307.0 7.0 %collective-permute-start.29 = (bf16[96,1280]{1,0:T(8,128)(2,1)S(1)}, bf16[96,1280]{1,0:T(8,128)(2,1)S(1)}, u32[]{:S(2)}, u32[]{:S(2)}) collective-permute-start(bf16[96,1280]{1,0:T(8,128)(2,1)S(1)} %fusion.14), channel_id=1, source_target_pairs={{0,16},{8,24},{16,0},{24,8},{1,17},{9,25},{17,1},{25,9},{2,18},{10... | collective-permute-start | bytes 737288 | tf_op jit(solution)/shard_map/ppermute | solution.py:389
  (18 other events, 107.3 us)
